TPU v7x, 512 devices: a whole 4x4x16 slice. The times are simulated.
512 devices in a mesh: row: 16 (over z_lo, x), col: 32 (over y, z_hi, core).
Axes of the slice: x: 4, y: 4, z: 16 (z_hi: 4, z_lo: 4; z = z_hi * 4 + z_lo), core: 2. Of those that a mesh axis runs over, the one named last changes fastest.
Arguments:
- x_cols: bfloat16 [8, 262144], P(None, ('col', 'row')), may hold values from -6 to 6
- diag_rows: float32 [262144], P(('row', 'col')), may hold values from 0.5 to 2
- theta: float32 [8], replicated, may hold values from -1 to 1
- tiles: bfloat16 [16, 32, 96, 128, 128], P('row', 'col'), may hold values from -0.109375 to 0.109375
- tile_rows: int32 [16, 32, 96], P('row', 'col'), may hold values from 0 to 127, as said below
- tile_cols: int32 [16, 32, 96], P('row', 'col'), may hold values from 0 to 63, as said below
- counts: int32 [16, 32], P('row', 'col'), may hold values from 48 to 96, as said below
Outputs:
- resid: float32 [8, 262144], P(None, ('row', 'col'))
- image: float32 [8, 262144], P(None, ('col', 'row'))
Inputs may be any that keep to these rules, and one draw needn't show every extreme that they name: Within one device block, the pairs (tile_rows, tile_cols) of its 96 slots are all different. `tile_cols`: paired with tile_rows slot by slot. `counts`: slots at or past a block's count are unused and their tiles hold arbitrary values. Some block has all 96 slots in use.
All inputs are finite; a program needn't handle non-finite values.
Results may differ from a plain program's by a relative error of at most 0.0023.
Values may be sent and summed in bfloat16 or wider, within the bound.
No kernel may reach another device: no remote copies, remote signals or barrier semaphores. Data moves between devices by JAX's collectives and lax.ppermute only.
A program may use at most 64 MiB of HBM per device.

v0:
```python
import jax
import jax.numpy as jnp
from jax import lax
from jax.sharding import PartitionSpec as P


def flatten_blocks(blocks):
    return blocks.transpose(1, 0, 2).reshape(blocks.shape[1], -1)


def body(x_cols, diag_rows, theta, tiles, tile_rows, tile_cols, counts):
    row_devices = lax.axis_size("row")
    column_devices = lax.axis_size("col")
    fold_ratio = column_devices // row_devices
    vectors = x_cols.shape[0]
    own_states = x_cols.shape[1]
    blocks_here = tiles[0, 0]
    rows_here = tile_rows[0, 0]
    cols_here = tile_cols[0, 0]
    slot_count = blocks_here.shape[0]
    tile_width = blocks_here.shape[1]
    in_use = jnp.arange(slot_count, dtype=jnp.int32) < counts[0, 0]
    block_rows = own_states * column_devices // tile_width
    block_cols = own_states * row_devices // tile_width
    share_rows = own_states // tile_width
    column_vectors = lax.all_gather(x_cols, "row", axis=1, tiled=True)
    column_tiles = column_vectors.reshape(vectors, block_cols, tile_width).transpose(1, 0, 2)
    picked = jnp.take(column_tiles, cols_here, axis=0)
    products = jnp.einsum("kab,knb->kna", blocks_here, picked, preferred_element_type=jnp.float32)
    products = jnp.where(in_use[:, None, None], products, 0.0)
    partial_value = jax.ops.segment_sum(products, rows_here, num_segments=block_rows)
    on_diag = (lax.axis_index("row") == lax.axis_index("col") // fold_ratio).astype(jnp.float32)
    offset = lax.axis_index("col") % fold_ratio * block_cols
    shift_term = -theta[None, :, None] * column_tiles.astype(jnp.float32) * on_diag
    current = lax.dynamic_slice_in_dim(partial_value, offset, block_cols, 0)
    partial_value = lax.dynamic_update_slice_in_dim(partial_value, current + shift_term, offset, 0)
    scales = lax.all_gather(diag_rows, "col", axis=0, tiled=True)
    summed = lax.psum(partial_value, "col")
    scaled = (summed / scales.reshape(-1, 1, tile_width)).astype(jnp.bfloat16)
    resid_part = lax.dynamic_slice_in_dim(summed, lax.axis_index("col") * share_rows, share_rows, 0)
    picked_rows = jnp.take(scaled, rows_here, axis=0)
    transposed = jnp.einsum(
        "kab,kna->knb", blocks_here, picked_rows, preferred_element_type=jnp.float32
    )
    transposed = jnp.where(in_use[:, None, None], transposed, 0.0)
    partial_back = jax.ops.segment_sum(transposed, cols_here, num_segments=block_cols)
    image_part = lax.psum_scatter(partial_back, "row", scatter_dimension=0, tiled=True)
    return (flatten_blocks(resid_part), flatten_blocks(image_part))


def solution(mesh):
    return jax.shard_map(
        body,
        mesh=mesh,
        in_specs=(
            P(None, ("col", "row")),
            P(("row", "col")),
            P(),
            P("row", "col", None, None, None),
            P("row", "col", None),
            P("row", "col", None),
            P("row", "col"),
        ),
        out_specs=(P(None, ("row", "col")), P(None, ("col", "row"))),
        check_vma=False,
    )
```

profile of v0, /device:TPU:8, one launch (start us, length us, event | category | flops | bytes accessed | tf_op | source)
XLA Modules:
  0.0 519.2 jit_solution(790691710098318919)
XLA Ops:
  7.2 0.0 copy-start
  7.2 0.0 copy-start.4
  7.2 0.0 all-reduce.2.cloned.1.call-start
  7.2 44.6 %all_gather.6 = bf16[8,8192]{1,0:T(8,128)(2,1)S(1)} all-gather(bf16[8,512]{1,0:T(8,128)(2,1)} %param.7), channel_id=1, replica_groups=mesh['row'=16,'col'=32] {'row'}, dimensions={1}, use_global_device_ids=true | all-gather | bytes 139264 | tf_op jit(solution)/shard_map/all_gather | solution.py:26
  51.8 0.7 fusion.16
  53.1 0.7 compare_and_fusion.1
  53.8 0.7 neg.4
  54.5 0.7 gather_fusion
  55.1 0.0 copy-done
  55.1 0.0 copy-start.3
  55.2 2.5 fusion.4
  57.7 0.8 broadcast_in_dim.43
  58.5 0.0 copy-done.4
  58.5 10.8 %scatter_fusion = f32[128,8,128]{2,1,0:T(8,128)} fusion(f32[128,8,128]{2,1,0:T(8,128)} %broadcast_in_dim.43, s32[96]{0:T(128)S(1)} %bitcast.40, f32[96,8,128]{2,1,0:T(8,128)} %fusion.4), kind=kCustom, calls=%fused_computation.2 | custom fusion | flops 98304 | bytes 1180032 | tf_op jit(solution)/shard_map/scatter-add | solution.py:31
  69.3 0.0 copy-start.2
  69.3 1.8 add_dynamic-update-slice_fusion
  71.1 0.0 all-reduce.2.cloned.1.call-update
  71.1 0.0 reduce-scatter.2.cloned.1.call-start
  71.2 0.0 copy-done.3
  71.2 52.4 %all-gather = f32[32,1,512]{2,1,0:T(1,128)S(1)} all-gather(f32[1,1,512]{2,1,0:T(1,128)S(1)} %bitcast.39), channel_id=1, replica_groups=mesh['row'=16,'col'=32] {'col'}, dimensions={0}, use_global_device_ids=true | all-gather | bytes 67584 | tf_op jit(solution)/shard_map/all_gather | solution.py:37
  123.7 278.2 %all-reduce.2.cloned.1.call-done = f32[128,8,128]{2,1,0:T(8,128)} async-done(((f32[128,8,128]{2,1,0:T(8,128)}), f32[128,8,128]{2,1,0:T(8,128)}) %all-reduce.2.cloned.1.call-update) | async-done | bytes 524304 | tf_op jit(solution)/shard_map/psum | solution.py:38
  401.9 1.1 divide_convert_fusion
  403.0 1.3 gather_fusion.1
  404.3 2.7 fusion.7
  407.0 0.0 copy-done.2
  407.0 7.3 %scatter_fusion.1 = f32[64,8,128]{2,1,0:T(8,128)S(1)} fusion(f32[64,8,128]{2,1,0:T(8,128)S(1)} %broadcast_in_dim.48, s32[96]{0:T(128)S(1)} %bitcast.38, f32[96,8,128]{2,1,0:T(8,128)} %fusion.7), kind=kCustom, calls=%fused_computation.3 | custom fusion | flops 98304 | bytes 1180032 | tf_op jit(solution)/shard_map/scatter-add | solution.py:46
  414.3 0.0 copy-start.1
  414.3 0.7 copy-done.1
  415.0 0.0 reduce-scatter.2.cloned.1.call-update
  415.0 1.3 dynamic-slice_bitcast_fusion
  416.4 96.0 %reduce-scatter.2.cloned.1.call-done = f32[4,8,128]{2,1,0:T(8,128)} async-done(((f32[64,8,128]{2,1,0:T(8,128)}), f32[4,8,128]{2,1,0:T(8,128)}) %reduce-scatter.2.cloned.1.call-update) | async-done | bytes 16400 | tf_op jit(solution)/shard_map/reduce_scatter | solution.py:47
  (5 shorter events, 0.0 us)
Async XLA Ops:
  7.2 48.0 %copy-start = (bf16[1,1,96,128,128]{4,3,2,1,0:T(8,128)(2,1)S(1)}, bf16[1,1,96,128,128]{4,3,2,1,0:T(8,128)(2,1)}, u32[]{:S(2)}) copy-start(bf16[1,1,96,128,128]{4,3,2,1,0:T(8,128)(2,1)} %param.10) | copy-start | bytes 9437188
  7.2 51.3 %copy-start.4 = (s32[1,1,96]{2,1,0:T(1,128)S(1)}, s32[1,1,96]{2,1,0:T(1,128)}, u32[]{:S(2)}) copy-start(s32[1,1,96]{2,1,0:T(1,128)} %param.11) | copy-start | bytes 1156
  7.2 394.7 %all-reduce.2.cloned.1.call-start = ((), (), s32[]{:S(2)}) async-start(), calls=%async_computation.1 | async-start | bytes 1048576 | tf_op jit(solution)/shard_map/psum | solution.py:38
  55.1 16.0 %copy-start.3 = (f32[512]{0:T(512)S(1)}, f32[512]{0:T(512)}, u32[]{:S(2)}) copy-start(f32[512]{0:T(512)} %param.8) | copy-start | bytes 6148
  69.3 337.7 %copy-start.2 = (s32[1,1,96]{2,1,0:T(1,128)S(1)}, s32[1,1,96]{2,1,0:T(1,128)}, u32[]{:S(2)}) copy-start(s32[1,1,96]{2,1,0:T(1,128)} %param.12) | copy-start | bytes 1156
  71.1 441.2 %reduce-scatter.2.cloned.1.call-start = ((), (), s32[]{:S(2)}) async-start(), calls=%async_computation.2 | async-start | bytes 278528 | tf_op jit(solution)/shard_map/reduce_scatter | solution.py:47
  414.3 0.7 copy-start.1
Sparse Core Ops, SparseCore 0:
  71.2 330.6 all-reduce.1
  415.2 97.1 reduce-scatter.1
where the time goes:
time: 520 us; the launch traced here: 519 us
  waiting for transfers between devices  374 us (72%)
  blocking collectives  97 us (19%)
  other arithmetic  23 us (4%)
  between operations  14.8 us (3%)
    psum x1, waiting for transfers between devices, body(): summed = lax.psum(partial_value, 'col')  278 us
    reduce_scatter x1, waiting for transfers between devices, body(): lax.psum_scatter(partial_back, 'row', scatter_dimension=0, tiled=True)  96 us
    all_gather x1, blocking collectives, body(): scales = lax.all_gather(diag_rows, 'col', axis=0, tiled=True)  52.4 us
    all_gather x1, blocking collectives, body(): column_vectors = lax.all_gather(x_cols, 'row', axis=1, tiled=True)  44.6 us
    scatter-add x1, other arithmetic, body(): jax.ops.segment_sum(products, rows_here, num_segments=block_rows)  10.8 us
  transfers between devices with their start and end apart: 2, of which 2 were waited for; matrix products, arithmetic and copies ran while one was open for 0% of the time, Pallas kernels for 0%

commit v1 on v0

v1 whole, which is shorter than its diff:
```python
import functools

import jax
import jax.numpy as jnp
from jax import lax
from jax.experimental import pallas as pl
from jax.experimental.pallas import tpu as pltpu
from jax.sharding import PartitionSpec as P

UNROLL = 8
COL_STEPS = (1, 8, 24, 2, 6)
ROW_STEPS = (1, 3, 4, 8)


def col_place(d):
    b = [(d >> i) & 1 for i in range(5)]
    return b[0] * 16 + (b[3] ^ b[4]) * 8 + b[4] * 4 + (b[1] ^ b[2]) * 2 + b[2]


def row_place(d):
    b = [(d >> i) & 1 for i in range(4)]
    return (b[0] ^ b[1]) * 8 + b[1] * 4 + b[2] * 2 + b[3]


def forward(me_ref, at_ref, from_ref, tiles_ref, x_ref, theta_ref, out_ref, total):
    share = 4
    total[...] = jnp.zeros_like(total)
    row, col = me_ref[0], me_ref[1]

    @pl.when(row == col // 2)
    def _():
        theta = theta_ref[...]
        first = (col % 2) * 16

        def shift(s, carry):
            q = row_place(s ^ row) * share
            p = col_place((first + s) ^ col) * share
            for j in range(share):
                total[p + j] = -theta * x_ref[q + j].astype(jnp.float32)
            return carry

        lax.fori_loop(0, 16, shift, 0)

    def step(i, carry):
        for u in range(UNROLL):
            k = i * UNROLL + u
            part = lax.dot_general(
                x_ref[from_ref[k]],
                tiles_ref[k],
                (((1,), (1,)), ((), ())),
                preferred_element_type=jnp.float32,
            )
            p = at_ref[k]
            total[p] = total[p] + part
        return carry

    lax.fori_loop(0, me_ref[2], step, 0)
    n = out_ref.shape[0]
    out_ref[...] = total[:n]


def backward(me_ref, from_ref, at_ref, tiles_ref, scaled_ref, out_ref, total):
    total[...] = jnp.zeros_like(total)

    def step(i, carry):
        for u in range(UNROLL):
            k = i * UNROLL + u
            part = jnp.dot(
                scaled_ref[from_ref[k]],
                tiles_ref[k],
                preferred_element_type=jnp.float32,
            )
            q = at_ref[k]
            total[q] = total[q] + part
        return carry

    lax.fori_loop(0, me_ref[2], step, 0)
    n = out_ref.shape[0]
    out_ref[...] = total[:n]


def swap(value, axis, step):
    n = lax.axis_size(axis)
    return lax.ppermute(value, axis, [(i, i ^ step) for i in range(n)])


def gather(own, axis, steps):
    for step in reversed(steps):
        own = jnp.concatenate([own, swap(own, axis, step)], axis=0)
    return own


def scatter_sum(parts, axis, steps):
    for step in steps:
        half = parts.shape[0] // 2
        parts = parts[:half] + swap(parts[half:], axis, step)
    return parts


def blocks_of(vectors):
    return vectors.reshape(vectors.shape[0], -1, 128).transpose(1, 0, 2)


def vectors_of(blocks):
    return blocks.transpose(1, 0, 2).reshape(blocks.shape[1], -1)


def body(x_cols, diag_rows, theta, tiles, tile_rows, tile_cols, counts):
    row, col = lax.axis_index("row"), lax.axis_index("col")
    tiles = tiles[0, 0]
    rows, cols, count = tile_rows[0, 0], tile_cols[0, 0], counts[0, 0]
    slots, width = tiles.shape[0], tiles.shape[1]
    used = jnp.arange(slots, dtype=jnp.int32) < count
    row_at = col_place((rows // 4) ^ col) * 4 + rows % 4
    col_at = row_place((cols // 4) ^ row) * 4 + cols % 4
    row_sum_at = jnp.where(used, row_at, 128)
    col_sum_at = jnp.where(used, col_at, 64)
    me = jnp.stack([row, col, (count + UNROLL - 1) // UNROLL]).astype(jnp.int32)
    smem = pl.BlockSpec(memory_space=pltpu.SMEM)
    vmem = pl.BlockSpec(memory_space=pltpu.VMEM)
    params = pltpu.CompilerParams(vmem_limit_bytes=24 * 1024 * 1024)
    cost = pl.CostEstimate(flops=2 * slots * 8 * width * width, bytes_accessed=4 << 20, transcendentals=0)

    x_all = gather(blocks_of(x_cols), "row", ROW_STEPS)
    partial = pl.pallas_call(
        forward,
        out_shape=jax.ShapeDtypeStruct((128, 8, width), jnp.float32),
        in_specs=[smem, smem, smem, vmem, vmem, vmem],
        out_specs=vmem,
        scratch_shapes=[pltpu.VMEM((136, 8, width), jnp.float32)],
        compiler_params=params,
        cost_estimate=cost,
    )(me, row_sum_at, col_at, tiles, x_all, jnp.broadcast_to(theta[:, None], (8, width)))
    resid = scatter_sum(partial, "col", COL_STEPS)
    scaled = (resid / diag_rows.reshape(-1, 1, width)).astype(jnp.bfloat16)
    scaled_all = gather(scaled, "col", COL_STEPS)
    back = pl.pallas_call(
        backward,
        out_shape=jax.ShapeDtypeStruct((64, 8, width), jnp.float32),
        in_specs=[smem, smem, smem, vmem, vmem],
        out_specs=vmem,
        scratch_shapes=[pltpu.VMEM((72, 8, width), jnp.float32)],
        compiler_params=params,
        cost_estimate=cost,
    )(me, row_at, col_sum_at, tiles, scaled_all)
    image = scatter_sum(back, "row", ROW_STEPS)
    return vectors_of(resid), vectors_of(image)


def solution(mesh):
    return jax.shard_map(
        body,
        mesh=mesh,
        in_specs=(
            P(None, ("col", "row")),
            P(("row", "col")),
            P(),
            P("row", "col", None, None, None),
            P("row", "col", None),
            P("row", "col", None),
            P("row", "col"),
        ),
        out_specs=(P(None, ("row", "col")), P(None, ("col", "row"))),
        check_vma=False,
    )
```

time: 520 us -> 144 us (0.28)
  the two profiles are of different devices: /device:TPU:8 before, /device:TPU:30 now
where the time goes in v1:
time: 144 us; the launch traced here: 143 us
  starting transfers between devices  70.7 us (49%)
  waiting for transfers between devices  57.7 us (40%)
  Pallas kernels  5.2 us (4%)
  other arithmetic  4.24 us (3%)
  local copies, waits for them, and re-layouts  3.52 us (2%)
  between operations  1.58 us (1%)
    ppermute x18, starting transfers between devices, swap(): return lax.ppermute(value, axis, [(i, i ^ step) for i in range(n)])  70.7 us
    ppermute x18, waiting for transfers between devices, swap(): return lax.ppermute(value, axis, [(i, i ^ step) for i in range(n)])  57.7 us
    pallas_call x1, Pallas kernels, body(): pl.pallas_call(forward, out_shape=jax.ShapeDtypeStruct((128, 8, width), j...  2.92 us
  transfers between devices with their start and end apart: 18, of which 17 were waited for; matrix products, arithmetic and copies ran while one was open for 2% of the time, Pallas kernels for 0%

profile of v1, /device:TPU:30, one launch (start us, length us, event | category | flops | bytes accessed | tf_op | source)
XLA Modules:
  0.0 142.9 jit_solution(454228666636412884)
XLA Ops:
  0.6 5.2 %collective-permute-start = (bf16[4,8,128]{2,1,0:T(8,128)(2,1)}, bf16[4,8,128]{2,1,0:T(8,128)(2,1)S(1)}, u32[]{:S(2)}, u32[]{:S(2)}) collective-permute-start(bf16[4,8,128]{2,1,0:T(8,128)(2,1)} %bitcast.50), channel_id=1, source_target_pairs={{0,256},{32,288},{64,320},{96,352},{128,384},{160,416},{192,448},{... | collective-permute-start | bytes 24584 | tf_op jit(solution)/shard_map/ppermute | solution.py:84
  8.7 3.8 %collective-permute-start.1 = (bf16[8,8,128]{2,1,0:T(8,128)(2,1)S(1)}, bf16[8,8,128]{2,1,0:T(8,128)(2,1)S(1)}, u32[]{:S(2)}, u32[]{:S(2)}) collective-permute-start(bf16[8,8,128]{2,1,0:T(8,128)(2,1)S(1)} %pad_maximum_fusion.4), channel_id=1, source_target_pairs={{0,128},{32,160},{64,192},{96,224},{128,0},{160,32},{192,64},{224,... | collective-permute-start | bytes 49160 | tf_op jit(solution)/shard_map/ppermute | solution.py:84
  15.0 2.4 %collective-permute-start.2 = (bf16[16,8,128]{2,1,0:T(8,128)(2,1)S(1)}, bf16[16,8,128]{2,1,0:T(8,128)(2,1)S(1)}, u32[]{:S(2)}, u32[]{:S(2)}) collective-permute-start(bf16[16,8,128]{2,1,0:T(8,128)(2,1)S(1)} %pad_maximum_fusion.2), channel_id=1, source_target_pairs={{0,96},{32,64},{64,32},{96,0},{128,224},{160,192},{192,160},{224,1... | collective-permute-start | bytes 98312 | tf_op jit(solution)/shard_map/ppermute | solution.py:84
  17.4 4.6 %collective-permute-done.2 = bf16[16,8,128]{2,1,0:T(8,128)(2,1)S(1)} collective-permute-done((bf16[16,8,128]{2,1,0:T(8,128)(2,1)S(1)}, bf16[16,8,128]{2,1,0:T(8,128)(2,1)S(1)}, u32[]{:S(2)}, u32[]{:S(2)}) %collective-permute-start.2) | collective-permute-done | bytes 32800 | tf_op jit(solution)/shard_map/ppermute | solution.py:84
  22.7 1.9 %collective-permute-start.3 = (bf16[32,8,128]{2,1,0:T(8,128)(2,1)S(1)}, bf16[32,8,128]{2,1,0:T(8,128)(2,1)S(1)}, u32[]{:S(2)}, u32[]{:S(2)}) collective-permute-start(bf16[32,8,128]{2,1,0:T(8,128)(2,1)S(1)} %pad_maximum_fusion), channel_id=1, source_target_pairs={{0,32},{32,0},{64,96},{96,64},{128,160},{160,128},{192,224},{224,1... | collective-permute-start | bytes 196616 | tf_op jit(solution)/shard_map/ppermute | solution.py:84
  24.6 4.2 %collective-permute-done.3 = bf16[32,8,128]{2,1,0:T(8,128)(2,1)S(1)} collective-permute-done((bf16[32,8,128]{2,1,0:T(8,128)(2,1)S(1)}, bf16[32,8,128]{2,1,0:T(8,128)(2,1)S(1)}, u32[]{:S(2)}, u32[]{:S(2)}) %collective-permute-start.3) | collective-permute-done | bytes 65568 | tf_op jit(solution)/shard_map/ppermute | solution.py:84
  29.6 1.9 %copy-done = bf16[1,1,96,128,128]{4,3,2,1,0:T(8,128)(2,1)S(1)} copy-done((bf16[1,1,96,128,128]{4,3,2,1,0:T(8,128)(2,1)S(1)}, bf16[1,1,96,128,128]{4,3,2,1,0:T(8,128)(2,1)}, u32[]{:S(2)}) %copy-start) | copy-done | bytes 3145752
  31.5 2.9 %shard_map.86 = f32[128,8,128]{2,1,0:T(8,128)S(1)} custom-call(s32[3]{0:T(128)S(1)} %pad_add_fusion.me_ref, s32[96]{0:T(128)S(1)} %get-tuple-element.16.at_ref, s32[96]{0:T(128)S(1)} %get-tuple-element.5.from_ref, bf16[96,128,128]{2,1,0:T(8,128)(2,1)S(1)} %bitcast.48, bf16[64,8,128]{2,1,0:T(8,128)(2,1)S(1)} %constant_dynamic-update-slice_fusion.x_ref, ...), custom_call_target="tpu_custom_call" | custom-call | flops 25165824 | bytes 4194304 | tf_op jit(solution)/shard_map/pallas_call | solution.py:125
  34.4 1.9 %collective-permute-start.4 = (f32[64,8,128]{2,1,0:T(8,128)S(1)}, f32[64,8,128]{2,1,0:T(8,128)S(1)}, u32[]{:S(2)}, u32[]{:S(2)}) collective-permute-start(f32[64,8,128]{2,1,0:T(8,128)S(1)} %slice.73), channel_id=1, source_target_pairs={{0,1},{1,0},{2,3},{3,2},{4,5},{5,4},{6,7},{7,6},{8,9},{9,8},{10,11... | collective-permute-start | bytes 786440 | tf_op jit(solution)/shard_map/ppermute | solution.py:84
  37.9 3.4 %collective-permute-start.5 = (f32[32,8,128]{2,1,0:T(8,128)S(1)}, f32[32,8,128]{2,1,0:T(8,128)S(1)}, u32[]{:S(2)}, u32[]{:S(2)}) collective-permute-start(f32[32,8,128]{2,1,0:T(8,128)S(1)} %slice.75), channel_id=1, source_target_pairs={{0,8},{1,9},{2,10},{3,11},{4,12},{5,13},{6,14},{7,15},{8,0},{9,1},... | collective-permute-start | bytes 393224 | tf_op jit(solution)/shard_map/ppermute | solution.py:84
  41.3 4.0 %collective-permute-done.5 = f32[32,8,128]{2,1,0:T(8,128)S(1)} collective-permute-done((f32[32,8,128]{2,1,0:T(8,128)S(1)}, f32[32,8,128]{2,1,0:T(8,128)S(1)}, u32[]{:S(2)}, u32[]{:S(2)}) %collective-permute-start.5) | collective-permute-done | bytes 131104 | tf_op jit(solution)/shard_map/ppermute | solution.py:84
  45.4 4.8 %collective-permute-start.6 = (f32[16,8,128]{2,1,0:T(8,128)S(1)}, f32[16,8,128]{2,1,0:T(8,128)S(1)}, u32[]{:S(2)}, u32[]{:S(2)}) collective-permute-start(f32[16,8,128]{2,1,0:T(8,128)S(1)} %slice.77), channel_id=1, source_target_pairs={{0,24},{1,25},{2,26},{3,27},{4,28},{5,29},{6,30},{7,31},{8,16},{9,... | collective-permute-start | bytes 196616 | tf_op jit(solution)/shard_map/ppermute | solution.py:84
  50.2 2.5 %collective-permute-done.6 = f32[16,8,128]{2,1,0:T(8,128)S(1)} collective-permute-done((f32[16,8,128]{2,1,0:T(8,128)S(1)}, f32[16,8,128]{2,1,0:T(8,128)S(1)}, u32[]{:S(2)}, u32[]{:S(2)}) %collective-permute-start.6) | collective-permute-done | bytes 65568 | tf_op jit(solution)/shard_map/ppermute | solution.py:84
  52.8 9.8 %collective-permute-start.7 = (f32[8,8,128]{2,1,0:T(8,128)S(1)}, f32[8,8,128]{2,1,0:T(8,128)S(1)}, u32[]{:S(2)}, u32[]{:S(2)}) collective-permute-start(f32[8,8,128]{2,1,0:T(8,128)S(1)} %slice.79), channel_id=1, source_target_pairs={{0,2},{1,3},{2,0},{3,1},{4,6},{5,7},{6,4},{7,5},{8,10},{9,11},{10,... | collective-permute-start | bytes 98312 | tf_op jit(solution)/shard_map/ppermute | solution.py:84
  64.5 10.6 %collective-permute-start.8 = (f32[4,8,128]{2,1,0:T(8,128)S(1)}, f32[4,8,128]{2,1,0:T(8,128)S(1)}, u32[]{:S(2)}, u32[]{:S(2)}) collective-permute-start(f32[4,8,128]{2,1,0:T(8,128)S(1)} %slice.81), channel_id=1, source_target_pairs={{0,6},{1,7},{2,4},{3,5},{4,2},{5,3},{6,0},{7,1},{8,14},{9,15},{10,... | collective-permute-start | bytes 49160 | tf_op jit(solution)/shard_map/ppermute | solution.py:84
  76.8 7.9 %collective-permute-start.9 = (bf16[4,8,128]{2,1,0:T(8,128)(2,1)S(1)}, bf16[4,8,128]{2,1,0:T(8,128)(2,1)S(1)}, u32[]{:S(2)}, u32[]{:S(2)}) collective-permute-start(bf16[4,8,128]{2,1,0:T(8,128)(2,1)S(1)} %get-tuple-element.3), channel_id=1, source_target_pairs={{0,6},{1,7},{2,4},{3,5},{4,2},{5,3},{6,0},{7,1},{8,14},{9,15},{10,... | collective-permute-start | bytes 24584 | tf_op jit(solution)/shard_map/ppermute | solution.py:84
  86.4 5.1 %collective-permute-start.10 = (bf16[8,8,128]{2,1,0:T(8,128)(2,1)S(1)}, bf16[8,8,128]{2,1,0:T(8,128)(2,1)S(1)}, u32[]{:S(2)}, u32[]{:S(2)}) collective-permute-start(bf16[8,8,128]{2,1,0:T(8,128)(2,1)S(1)} %pad_maximum_fusion.5), channel_id=1, source_target_pairs={{0,2},{1,3},{2,0},{3,1},{4,6},{5,7},{6,4},{7,5},{8,10},{9,11},{10,... | collective-permute-start | bytes 49160 | tf_op jit(solution)/shard_map/ppermute | solution.py:84
  91.5 4.4 %collective-permute-done.10 = bf16[8,8,128]{2,1,0:T(8,128)(2,1)S(1)} collective-permute-done((bf16[8,8,128]{2,1,0:T(8,128)(2,1)S(1)}, bf16[8,8,128]{2,1,0:T(8,128)(2,1)S(1)}, u32[]{:S(2)}, u32[]{:S(2)}) %collective-permute-start.10) | collective-permute-done | bytes 16416 | tf_op jit(solution)/shard_map/ppermute | solution.py:84
  95.9 1.9 %collective-permute-start.11 = (bf16[16,8,128]{2,1,0:T(8,128)(2,1)S(1)}, bf16[16,8,128]{2,1,0:T(8,128)(2,1)S(1)}, u32[]{:S(2)}, u32[]{:S(2)}) collective-permute-start(bf16[16,8,128]{2,1,0:T(8,128)(2,1)S(1)} %pad_maximum_fusion.3), channel_id=1, source_target_pairs={{0,24},{1,25},{2,26},{3,27},{4,28},{5,29},{6,30},{7,31},{8,16},{9,... | collective-permute-start | bytes 98312 | tf_op jit(solution)/shard_map/ppermute | solution.py:84
  97.8 5.1 %collective-permute-done.11 = bf16[16,8,128]{2,1,0:T(8,128)(2,1)S(1)} collective-permute-done((bf16[16,8,128]{2,1,0:T(8,128)(2,1)S(1)}, bf16[16,8,128]{2,1,0:T(8,128)(2,1)S(1)}, u32[]{:S(2)}, u32[]{:S(2)}) %collective-permute-start.11) | collective-permute-done | bytes 32800 | tf_op jit(solution)/shard_map/ppermute | solution.py:84
  102.9 1.9 %collective-permute-start.12 = (bf16[32,8,128]{2,1,0:T(8,128)(2,1)S(1)}, bf16[32,8,128]{2,1,0:T(8,128)(2,1)S(1)}, u32[]{:S(2)}, u32[]{:S(2)}) collective-permute-start(bf16[32,8,128]{2,1,0:T(8,128)(2,1)S(1)} %pad_maximum_fusion.1), channel_id=1, source_target_pairs={{0,8},{1,9},{2,10},{3,11},{4,12},{5,13},{6,14},{7,15},{8,0},{9,1},... | collective-permute-start | bytes 196616 | tf_op jit(solution)/shard_map/ppermute | solution.py:84
  104.9 4.2 %collective-permute-done.12 = bf16[32,8,128]{2,1,0:T(8,128)(2,1)S(1)} collective-permute-done((bf16[32,8,128]{2,1,0:T(8,128)(2,1)S(1)}, bf16[32,8,128]{2,1,0:T(8,128)(2,1)S(1)}, u32[]{:S(2)}, u32[]{:S(2)}) %collective-permute-start.12) | collective-permute-done | bytes 65568 | tf_op jit(solution)/shard_map/ppermute | solution.py:84
  109.1 1.9 %collective-permute-start.13 = (bf16[64,8,128]{2,1,0:T(8,128)(2,1)S(1)}, bf16[64,8,128]{2,1,0:T(8,128)(2,1)S(1)}, u32[]{:S(2)}, u32[]{:S(2)}) collective-permute-start(bf16[64,8,128]{2,1,0:T(8,128)(2,1)S(1)} %get-tuple-element.8), channel_id=1, source_target_pairs={{0,1},{1,0},{2,3},{3,2},{4,5},{5,4},{6,7},{7,6},{8,9},{9,8},{10,11... | collective-permute-start | bytes 393224 | tf_op jit(solution)/shard_map/ppermute | solution.py:84
  112.4 2.3 %shard_map.87 = f32[64,8,128]{2,1,0:T(8,128)S(1)} custom-call(s32[3]{0:T(128)S(1)} %pad_add_fusion.me_ref, s32[96]{0:T(128)S(1)} %get-tuple-element.17.from_ref, s32[96]{0:T(128)S(1)} %get-tuple-element.4.at_ref, bf16[96,128,128]{2,1,0:T(8,128)(2,1)S(1)} %bitcast.49, bf16[128,8,128]{2,1,0:T(8,128)(2,1)S(1)} %constant_dynamic-update-slice_fusion.10.scaled_ref), custom_call_target="tpu_custom_call" | custom-call | flops 25165824 | bytes 4194304 | tf_op jit(solution)/shard_map/pallas_call | solution.py:137
  114.7 1.9 %collective-permute-start.14 = (f32[32,8,128]{2,1,0:T(8,128)S(1)}, f32[32,8,128]{2,1,0:T(8,128)S(1)}, u32[]{:S(2)}, u32[]{:S(2)}) collective-permute-start(f32[32,8,128]{2,1,0:T(8,128)S(1)} %slice.83), channel_id=1, source_target_pairs={{0,32},{32,0},{64,96},{96,64},{128,160},{160,128},{192,224},{224,1... | collective-permute-start | bytes 393224 | tf_op jit(solution)/shard_map/ppermute | solution.py:84
  116.6 5.9 %collective-permute-done.14 = f32[32,8,128]{2,1,0:T(8,128)S(1)} collective-permute-done((f32[32,8,128]{2,1,0:T(8,128)S(1)}, f32[32,8,128]{2,1,0:T(8,128)S(1)}, u32[]{:S(2)}, u32[]{:S(2)}) %collective-permute-start.14) | collective-permute-done | bytes 131104 | tf_op jit(solution)/shard_map/ppermute | solution.py:84
  122.6 1.9 %collective-permute-start.15 = (f32[16,8,128]{2,1,0:T(8,128)S(1)}, f32[16,8,128]{2,1,0:T(8,128)S(1)}, u32[]{:S(2)}, u32[]{:S(2)}) collective-permute-start(f32[16,8,128]{2,1,0:T(8,128)S(1)} %slice.85), channel_id=1, source_target_pairs={{0,96},{32,64},{64,32},{96,0},{128,224},{160,192},{192,160},{224,1... | collective-permute-start | bytes 196616 | tf_op jit(solution)/shard_map/ppermute | solution.py:84
  124.5 5.4 %collective-permute-done.15 = f32[16,8,128]{2,1,0:T(8,128)S(1)} collective-permute-done((f32[16,8,128]{2,1,0:T(8,128)S(1)}, f32[16,8,128]{2,1,0:T(8,128)S(1)}, u32[]{:S(2)}, u32[]{:S(2)}) %collective-permute-start.15) | collective-permute-done | bytes 65568 | tf_op jit(solution)/shard_map/ppermute | solution.py:84
  130.0 2.2 %collective-permute-start.16 = (f32[8,8,128]{2,1,0:T(8,128)S(1)}, f32[8,8,128]{2,1,0:T(8,128)S(1)}, u32[]{:S(2)}, u32[]{:S(2)}) collective-permute-start(f32[8,8,128]{2,1,0:T(8,128)S(1)} %slice.87), channel_id=1, source_target_pairs={{0,128},{32,160},{64,192},{96,224},{128,0},{160,32},{192,64},{224,... | collective-permute-start | bytes 98312 | tf_op jit(solution)/shard_map/ppermute | solution.py:84
  132.2 3.6 %collective-permute-done.16 = f32[8,8,128]{2,1,0:T(8,128)S(1)} collective-permute-done((f32[8,8,128]{2,1,0:T(8,128)S(1)}, f32[8,8,128]{2,1,0:T(8,128)S(1)}, u32[]{:S(2)}, u32[]{:S(2)}) %collective-permute-start.16) | collective-permute-done | bytes 32800 | tf_op jit(solution)/shard_map/ppermute | solution.py:84
  135.8 2.0 %collective-permute-start.17 = (f32[4,8,128]{2,1,0:T(8,128)S(1)}, f32[4,8,128]{2,1,0:T(8,128)S(1)}, u32[]{:S(2)}, u32[]{:S(2)}) collective-permute-start(f32[4,8,128]{2,1,0:T(8,128)S(1)} %slice.89), channel_id=1, source_target_pairs={{0,256},{32,288},{64,320},{96,352},{128,384},{160,416},{192,448},{... | collective-permute-start | bytes 49160 | tf_op jit(solution)/shard_map/ppermute | solution.py:84
  138.4 3.9 %collective-permute-done.17 = f32[4,8,128]{2,1,0:T(8,128)S(1)} collective-permute-done((f32[4,8,128]{2,1,0:T(8,128)S(1)}, f32[4,8,128]{2,1,0:T(8,128)S(1)}, u32[]{:S(2)}, u32[]{:S(2)}) %collective-permute-start.17) | collective-permute-done | bytes 16416 | tf_op jit(solution)/shard_map/ppermute | solution.py:84
  (51 shorter events, 15.7 us)
Async XLA Ops:
  0.6 7.3 %collective-permute-start = (bf16[4,8,128]{2,1,0:T(8,128)(2,1)}, bf16[4,8,128]{2,1,0:T(8,128)(2,1)S(1)}, u32[]{:S(2)}, u32[]{:S(2)}) collective-permute-start(bf16[4,8,128]{2,1,0:T(8,128)(2,1)} %bitcast.50), channel_id=1, source_target_pairs={{0,256},{32,288},{64,320},{96,352},{128,384},{160,416},{192,448},{... | collective-permute-start | bytes 24584 | tf_op jit(solution)/shard_map/ppermute | solution.py:84
  8.7 5.6 %collective-permute-start.1 = (bf16[8,8,128]{2,1,0:T(8,128)(2,1)S(1)}, bf16[8,8,128]{2,1,0:T(8,128)(2,1)S(1)}, u32[]{:S(2)}, u32[]{:S(2)}) collective-permute-start(bf16[8,8,128]{2,1,0:T(8,128)(2,1)S(1)} %pad_maximum_fusion.4), channel_id=1, source_target_pairs={{0,128},{32,160},{64,192},{96,224},{128,0},{160,32},{192,64},{224,... | collective-permute-start | bytes 49160 | tf_op jit(solution)/shard_map/ppermute | solution.py:84
  15.0 7.0 %collective-permute-start.2 = (bf16[16,8,128]{2,1,0:T(8,128)(2,1)S(1)}, bf16[16,8,128]{2,1,0:T(8,128)(2,1)S(1)}, u32[]{:S(2)}, u32[]{:S(2)}) collective-permute-start(bf16[16,8,128]{2,1,0:T(8,128)(2,1)S(1)} %pad_maximum_fusion.2), channel_id=1, source_target_pairs={{0,96},{32,64},{64,32},{96,0},{128,224},{160,192},{192,160},{224,1... | collective-permute-start | bytes 98312 | tf_op jit(solution)/shard_map/ppermute | solution.py:84
  22.7 6.2 %collective-permute-start.3 = (bf16[32,8,128]{2,1,0:T(8,128)(2,1)S(1)}, bf16[32,8,128]{2,1,0:T(8,128)(2,1)S(1)}, u32[]{:S(2)}, u32[]{:S(2)}) collective-permute-start(bf16[32,8,128]{2,1,0:T(8,128)(2,1)S(1)} %pad_maximum_fusion), channel_id=1, source_target_pairs={{0,32},{32,0},{64,96},{96,64},{128,160},{160,128},{192,224},{224,1... | collective-permute-start | bytes 196616 | tf_op jit(solution)/shard_map/ppermute | solution.py:84
  29.6 1.9 %copy-start = (bf16[1,1,96,128,128]{4,3,2,1,0:T(8,128)(2,1)S(1)}, bf16[1,1,96,128,128]{4,3,2,1,0:T(8,128)(2,1)}, u32[]{:S(2)}) copy-start(bf16[1,1,96,128,128]{4,3,2,1,0:T(8,128)(2,1)} %param.10) | copy-start | bytes 9437188
  31.5 45.3 %copy-start.2 = (f32[512]{0:T(512)S(1)}, f32[512]{0:T(512)}, u32[]{:S(2)}) copy-start(f32[512]{0:T(512)} %param.8) | copy-start | bytes 6148
  31.5 80.9 %copy-start.1 = (bf16[1,1,96,128,128]{4,3,2,1,0:T(8,128)(2,1)S(1)}, bf16[1,1,96,128,128]{4,3,2,1,0:T(8,128)(2,1)}, u32[]{:S(2)}) copy-start(bf16[1,1,96,128,128]{4,3,2,1,0:T(8,128)(2,1)} %param.10) | copy-start | bytes 9437188
  34.4 3.4 %collective-permute-start.4 = (f32[64,8,128]{2,1,0:T(8,128)S(1)}, f32[64,8,128]{2,1,0:T(8,128)S(1)}, u32[]{:S(2)}, u32[]{:S(2)}) collective-permute-start(f32[64,8,128]{2,1,0:T(8,128)S(1)} %slice.73), channel_id=1, source_target_pairs={{0,1},{1,0},{2,3},{3,2},{4,5},{5,4},{6,7},{7,6},{8,9},{9,8},{10,11... | collective-permute-start | bytes 786440 | tf_op jit(solution)/shard_map/ppermute | solution.py:84
  37.9 7.4 %collective-permute-start.5 = (f32[32,8,128]{2,1,0:T(8,128)S(1)}, f32[32,8,128]{2,1,0:T(8,128)S(1)}, u32[]{:S(2)}, u32[]{:S(2)}) collective-permute-start(f32[32,8,128]{2,1,0:T(8,128)S(1)} %slice.75), channel_id=1, source_target_pairs={{0,8},{1,9},{2,10},{3,11},{4,12},{5,13},{6,14},{7,15},{8,0},{9,1},... | collective-permute-start | bytes 393224 | tf_op jit(solution)/shard_map/ppermute | solution.py:84
  45.4 7.4 %collective-permute-start.6 = (f32[16,8,128]{2,1,0:T(8,128)S(1)}, f32[16,8,128]{2,1,0:T(8,128)S(1)}, u32[]{:S(2)}, u32[]{:S(2)}) collective-permute-start(f32[16,8,128]{2,1,0:T(8,128)S(1)} %slice.77), channel_id=1, source_target_pairs={{0,24},{1,25},{2,26},{3,27},{4,28},{5,29},{6,30},{7,31},{8,16},{9,... | collective-permute-start | bytes 196616 | tf_op jit(solution)/shard_map/ppermute | solution.py:84
  52.8 11.7 %collective-permute-start.7 = (f32[8,8,128]{2,1,0:T(8,128)S(1)}, f32[8,8,128]{2,1,0:T(8,128)S(1)}, u32[]{:S(2)}, u32[]{:S(2)}) collective-permute-start(f32[8,8,128]{2,1,0:T(8,128)S(1)} %slice.79), channel_id=1, source_target_pairs={{0,2},{1,3},{2,0},{3,1},{4,6},{5,7},{6,4},{7,5},{8,10},{9,11},{10,... | collective-permute-start | bytes 98312 | tf_op jit(solution)/shard_map/ppermute | solution.py:84
  64.5 12.3 %collective-permute-start.8 = (f32[4,8,128]{2,1,0:T(8,128)S(1)}, f32[4,8,128]{2,1,0:T(8,128)S(1)}, u32[]{:S(2)}, u32[]{:S(2)}) collective-permute-start(f32[4,8,128]{2,1,0:T(8,128)S(1)} %slice.81), channel_id=1, source_target_pairs={{0,6},{1,7},{2,4},{3,5},{4,2},{5,3},{6,0},{7,1},{8,14},{9,15},{10,... | collective-permute-start | bytes 49160 | tf_op jit(solution)/shard_map/ppermute | solution.py:84
  76.8 9.6 %collective-permute-start.9 = (bf16[4,8,128]{2,1,0:T(8,128)(2,1)S(1)}, bf16[4,8,128]{2,1,0:T(8,128)(2,1)S(1)}, u32[]{:S(2)}, u32[]{:S(2)}) collective-permute-start(bf16[4,8,128]{2,1,0:T(8,128)(2,1)S(1)} %get-tuple-element.3), channel_id=1, source_target_pairs={{0,6},{1,7},{2,4},{3,5},{4,2},{5,3},{6,0},{7,1},{8,14},{9,15},{10,... | collective-permute-start | bytes 24584 | tf_op jit(solution)/shard_map/ppermute | solution.py:84
  86.4 9.5 %collective-permute-start.10 = (bf16[8,8,128]{2,1,0:T(8,128)(2,1)S(1)}, bf16[8,8,128]{2,1,0:T(8,128)(2,1)S(1)}, u32[]{:S(2)}, u32[]{:S(2)}) collective-permute-start(bf16[8,8,128]{2,1,0:T(8,128)(2,1)S(1)} %pad_maximum_fusion.5), channel_id=1, source_target_pairs={{0,2},{1,3},{2,0},{3,1},{4,6},{5,7},{6,4},{7,5},{8,10},{9,11},{10,... | collective-permute-start | bytes 49160 | tf_op jit(solution)/shard_map/ppermute | solution.py:84
  95.9 7.0 %collective-permute-start.11 = (bf16[16,8,128]{2,1,0:T(8,128)(2,1)S(1)}, bf16[16,8,128]{2,1,0:T(8,128)(2,1)S(1)}, u32[]{:S(2)}, u32[]{:S(2)}) collective-permute-start(bf16[16,8,128]{2,1,0:T(8,128)(2,1)S(1)} %pad_maximum_fusion.3), channel_id=1, source_target_pairs={{0,24},{1,25},{2,26},{3,27},{4,28},{5,29},{6,30},{7,31},{8,16},{9,... | collective-permute-start | bytes 98312 | tf_op jit(solution)/shard_map/ppermute | solution.py:84
  102.9 6.2 %collective-permute-start.12 = (bf16[32,8,128]{2,1,0:T(8,128)(2,1)S(1)}, bf16[32,8,128]{2,1,0:T(8,128)(2,1)S(1)}, u32[]{:S(2)}, u32[]{:S(2)}) collective-permute-start(bf16[32,8,128]{2,1,0:T(8,128)(2,1)S(1)} %pad_maximum_fusion.1), channel_id=1, source_target_pairs={{0,8},{1,9},{2,10},{3,11},{4,12},{5,13},{6,14},{7,15},{8,0},{9,1},... | collective-permute-start | bytes 196616 | tf_op jit(solution)/shard_map/ppermute | solution.py:84
  109.1 3.2 %collective-permute-start.13 = (bf16[64,8,128]{2,1,0:T(8,128)(2,1)S(1)}, bf16[64,8,128]{2,1,0:T(8,128)(2,1)S(1)}, u32[]{:S(2)}, u32[]{:S(2)}) collective-permute-start(bf16[64,8,128]{2,1,0:T(8,128)(2,1)S(1)} %get-tuple-element.8), channel_id=1, source_target_pairs={{0,1},{1,0},{2,3},{3,2},{4,5},{5,4},{6,7},{7,6},{8,9},{9,8},{10,11... | collective-permute-start | bytes 393224 | tf_op jit(solution)/shard_map/ppermute | solution.py:84
  114.7 7.8 %collective-permute-start.14 = (f32[32,8,128]{2,1,0:T(8,128)S(1)}, f32[32,8,128]{2,1,0:T(8,128)S(1)}, u32[]{:S(2)}, u32[]{:S(2)}) collective-permute-start(f32[32,8,128]{2,1,0:T(8,128)S(1)} %slice.83), channel_id=1, source_target_pairs={{0,32},{32,0},{64,96},{96,64},{128,160},{160,128},{192,224},{224,1... | collective-permute-start | bytes 393224 | tf_op jit(solution)/shard_map/ppermute | solution.py:84
  122.6 7.4 %collective-permute-start.15 = (f32[16,8,128]{2,1,0:T(8,128)S(1)}, f32[16,8,128]{2,1,0:T(8,128)S(1)}, u32[]{:S(2)}, u32[]{:S(2)}) collective-permute-start(f32[16,8,128]{2,1,0:T(8,128)S(1)} %slice.85), channel_id=1, source_target_pairs={{0,96},{32,64},{64,32},{96,0},{128,224},{160,192},{192,160},{224,1... | collective-permute-start | bytes 196616 | tf_op jit(solution)/shard_map/ppermute | solution.py:84
  130.0 5.8 %collective-permute-start.16 = (f32[8,8,128]{2,1,0:T(8,128)S(1)}, f32[8,8,128]{2,1,0:T(8,128)S(1)}, u32[]{:S(2)}, u32[]{:S(2)}) collective-permute-start(f32[8,8,128]{2,1,0:T(8,128)S(1)} %slice.87), channel_id=1, source_target_pairs={{0,128},{32,160},{64,192},{96,224},{128,0},{160,32},{192,64},{224,... | collective-permute-start | bytes 98312 | tf_op jit(solution)/shard_map/ppermute | solution.py:84
  135.8 6.5 %collective-permute-start.17 = (f32[4,8,128]{2,1,0:T(8,128)S(1)}, f32[4,8,128]{2,1,0:T(8,128)S(1)}, u32[]{:S(2)}, u32[]{:S(2)}) collective-permute-start(f32[4,8,128]{2,1,0:T(8,128)S(1)} %slice.89), channel_id=1, source_target_pairs={{0,256},{32,288},{64,320},{96,352},{128,384},{160,416},{192,448},{... | collective-permute-start | bytes 49160 | tf_op jit(solution)/shard_map/ppermute | solution.py:84

commit v2 on v0

v2 whole, which is shorter than its diff:
```python
import functools

import jax
import jax.numpy as jnp
from jax import lax
from jax.experimental import pallas as pl
from jax.experimental.pallas import tpu as pltpu
from jax.sharding import Mesh, PartitionSpec as P

ROW = ("zl", "x")
COL = ("y", "zh", "c")
AT_ROW, AT_COL, AT_CORE = 96, 97, 98


def place(share, core):
    y, zh, c = share >> 3, (share >> 1) & 3, share & 1
    return ((c ^ core) << 4) | (y << 2) | zh


def prepare(tiles_ref, theta_ref, diag_ref, lines_ref, block_ref):
    line = lax.broadcasted_iota(jnp.int32, lines_ref.shape, 0)
    lines = jnp.zeros(lines_ref.shape, jnp.float32)
    for n in range(8):
        lines = jnp.where(line == n, theta_ref[n], lines)
    lines_ref[...] = lines
    block_ref[0, :4] = diag_ref[...]
    block_ref[0, 4:] = jnp.zeros((4, 128), jnp.float32)


def forward(table_ref, tiles_ref, lines_ref, x_ref, out_ref, total):
    total[...] = jnp.zeros_like(total)
    row, col = table_ref[AT_ROW], table_ref[AT_COL]

    @pl.when(row == col >> 1)
    def _():
        first = (col & 1) * 16

        def shift(s, carry):
            p = place(first + s, table_ref[AT_CORE]) * 4
            for j in range(4):
                total[p + j] = -lines_ref[...] * x_ref[s * 4 + j].astype(jnp.float32)
            return carry

        lax.fori_loop(0, 16, shift, 0)

    for i in range(48):
        v, w = table_ref[2 * i], table_ref[2 * i + 1]
        both = jnp.concatenate([x_ref[v & 63], x_ref[w & 63]], axis=0)
        part = lax.dot_general(
            both, tiles_ref[i], (((1,), (1,)), ((), ())), preferred_element_type=jnp.float32
        )
        total[v >> 8] = total[v >> 8] + part[:8, :128]
        total[w >> 8] = total[w >> 8] + part[8:, 128:]
    out_ref[...] = total[:128]


def backward(table_ref, tiles_ref, scaled_ref, out_ref, total):
    total[...] = jnp.zeros_like(total)
    for i in range(48):
        v, w = table_ref[2 * i], table_ref[2 * i + 1]
        a, b = scaled_ref[(v >> 8) & 127], scaled_ref[(w >> 8) & 127]
        none = jnp.zeros_like(a)
        both = jnp.concatenate(
            [jnp.concatenate([a, none], axis=0), jnp.concatenate([none, b], axis=0)], axis=1
        )
        part = jnp.dot(both, tiles_ref[i], preferred_element_type=jnp.float32)
        total[v & 255] = total[v & 255] + part[:8]
        total[w & 255] = total[w & 255] + part[8:]
    out_ref[...] = total[:64].astype(out_ref.dtype)


def swap_cores(value):
    return lax.ppermute(value, "c", [(0, 1), (1, 0)])


def to_all(own, axes):
    copies = jnp.broadcast_to(own[None], (lax.axis_size(axes), *own.shape))
    return lax.all_to_all(copies, axes, 0, 0)


def sum_shares(parts, axes):
    n = lax.axis_size(axes)
    parts = parts.reshape(n, parts.shape[0] // n, *parts.shape[1:])
    return jnp.sum(lax.all_to_all(parts, axes, 0, 0).astype(jnp.float32), axis=0)


def vectors_of(blocks):
    return blocks.transpose(1, 0, 2).reshape(blocks.shape[1], -1)


def body(x_cols, diag_rows, theta, tiles, tile_rows, tile_cols, counts):
    core = lax.axis_index("c")
    slots, width = tiles.shape[2], tiles.shape[3]
    rows = jnp.pad(tile_rows[0, 0], (0, 32))
    cols = jnp.pad(tile_cols[0, 0], (0, 32))
    slot = jnp.arange(slots + 32, dtype=jnp.int32)
    used = slot < counts[0, 0]
    table = jnp.where(used, ((place(rows >> 2, core) << 2) | (rows & 3)) << 8 | cols, 128 << 8 | 64)
    table = jnp.where(slot == AT_ROW, lax.axis_index(ROW), table)
    table = jnp.where(slot == AT_COL, lax.axis_index(COL), table)
    table = jnp.where(slot == AT_CORE, core, table).astype(jnp.int32)

    smem = pl.BlockSpec(memory_space=pltpu.SMEM)
    vmem = pl.BlockSpec(memory_space=pltpu.VMEM)
    params = pltpu.CompilerParams(vmem_limit_bytes=16 * 1024 * 1024)
    cost = pl.CostEstimate(flops=2 * slots * 8 * width * width, bytes_accessed=4 << 20, transcendentals=0)
    f32 = functools.partial(jax.ShapeDtypeStruct, dtype=jnp.float32)

    tiles_here = tiles.reshape(slots // 2, 2 * width, width)
    lines, diag_block = pl.pallas_call(
        prepare,
        out_shape=(f32((8, width)), f32((1, 8, width))),
        in_specs=[vmem, smem, vmem],
        out_specs=(vmem, vmem),
        compiler_params=params,
        cost_estimate=cost,
    )(tiles_here, theta, diag_rows.reshape(4, width))

    own = x_cols.reshape(8, 4, width).transpose(1, 0, 2)
    x_all = to_all(own, ROW).reshape(64, 8, width)
    partial = pl.pallas_call(
        forward,
        out_shape=f32((128, 8, width)),
        in_specs=[smem, vmem, vmem, vmem],
        out_specs=vmem,
        scratch_shapes=[pltpu.VMEM((136, 8, width), jnp.float32)],
        compiler_params=params,
        cost_estimate=cost,
    )(table, tiles_here, lines, x_all)

    partial = sum_shares(partial[:64] + swap_cores(partial[64:]), "y")
    got = to_all(jnp.concatenate([partial, diag_block], axis=0), "zh")
    resid = jnp.sum(got[:, :16], axis=0)
    diag = got[:, 16, :4].reshape(16, 1, width)
    scaled = to_all((resid / diag).astype(jnp.bfloat16), "y").reshape(64, 8, width)
    scaled = jnp.concatenate([scaled, swap_cores(scaled)], axis=0)

    back = pl.pallas_call(
        backward,
        out_shape=f32((64, 8, width)),
        in_specs=[smem, vmem, vmem],
        out_specs=vmem,
        scratch_shapes=[pltpu.VMEM((72, 8, width), jnp.float32)],
        compiler_params=params,
        cost_estimate=cost,
    )(table, tiles_here, scaled)
    image = sum_shares(back, ROW)
    resid = lax.dynamic_slice_in_dim(resid, lax.axis_index("zh") * 4, 4, 0)
    return vectors_of(resid), vectors_of(image)


def solution(mesh):
    fine = Mesh(mesh.devices.reshape(4, 4, 4, 4, 2), ROW + COL)
    return jax.shard_map(
        body,
        mesh=fine,
        in_specs=(
            P(None, COL + ROW),
            P(ROW + COL),
            P(),
            P(ROW, COL, None, None, None),
            P(ROW, COL, None),
            P(ROW, COL, None),
            P(ROW, COL),
        ),
        out_specs=(P(None, ROW + COL), P(None, COL + ROW)),
        check_vma=False,
    )
```

time: 520 us -> 98.8 us (0.19)
  the two profiles are of different devices: /device:TPU:8 before, /device:TPU:1 now
where the time goes in v2:
time: 98.8 us; the launch traced here: 98.2 us
  blocking collectives  45.4 us (46%)
  starting transfers between devices  26.4 us (27%)
  waiting for transfers between devices  14.8 us (15%)
  local copies, waits for them, and re-layouts  5.28 us (5%)
  Pallas kernels  4.14 us (4%)
  between operations  1.45 us (1%)
    all_to_all x2, blocking collectives, to_all(): return lax.all_to_all(copies, axes, 0, 0)  36.1 us
    ppermute x2, starting transfers between devices, swap_cores(): return lax.ppermute(value, 'c', [(0, 1), (1, 0)])  11.6 us
    all_to_all x1, blocking collectives, sum_shares(): lax.all_to_all(parts, axes, 0, 0).astype(jnp.float32)  9.27 us
    all_to_all x1, waiting for transfers between devices, sum_shares(): lax.all_to_all(parts, axes, 0, 0).astype(jnp.float32)  9.27 us
    all_to_all x1, starting transfers between devices, to_all(): return lax.all_to_all(copies, axes, 0, 0)  9.01 us
    all_to_all x1, starting transfers between devices, sum_shares(): lax.all_to_all(parts, axes, 0, 0).astype(jnp.float32)  5.79 us
    all_to_all x1, waiting for transfers between devices, to_all(): return lax.all_to_all(copies, axes, 0, 0)  3.41 us
    unnamed x12, local copies, waits for them, and re-layouts  3.23 us
  transfers between devices with their start and end apart: 4, of which 4 were waited for; matrix products, arithmetic and copies ran while one was open for 1% of the time, Pallas kernels for 1%

profile of v2, /device:TPU:1, one launch (start us, length us, event | category | flops | bytes accessed | tf_op | source)
XLA Modules:
  0.0 98.2 jit_solution(7229179699470355390)
XLA Ops:
  0.6 0.0 copy-start.4
  0.6 0.0 copy-start.5
  0.6 1.4 %broadcast_in_dim.36 = bf16[16,4,8,128]{3,2,1,0:T(8,128)(2,1)} broadcast(bf16[4,8,128]{2,1,0:T(8,128)(2,1)} %bitcast.31), dimensions={1,2,3} | broadcast | bytes 139264 | tf_op jit(solution)/shard_map/broadcast_in_dim | solution.py:77
  2.0 9.0 %all-to-all-start = ((bf16[16,4,8,128]{3,2,1,0:T(8,128)(2,1)}), bf16[16,4,8,128]{3,2,1,0:T(8,128)(2,1)S(1)}, u32[]{:S(2)}, u32[]{:S(2)}) async-start(bf16[16,4,8,128]{3,2,1,0:T(8,128)(2,1)} %broadcast_in_dim.36), calls=%async_computation | async-start | bytes 262144 | tf_op jit(solution)/shard_map/all_to_all | solution.py:78
  11.7 0.0 copy-start
  11.7 1.9 %copy-done = bf16[1,1,96,128,128]{4,3,2,1,0:T(8,128)(2,1)S(1)} copy-done((bf16[1,1,96,128,128]{4,3,2,1,0:T(8,128)(2,1)S(1)}, bf16[1,1,96,128,128]{4,3,2,1,0:T(8,128)(2,1)}, u32[]{:S(2)}) %copy-start) | copy-done | bytes 3145752
  13.6 0.0 copy-start.2
  13.6 0.7 copy-done.2
  14.3 0.0 copy-start.3
  14.3 0.7 copy-done.3
  14.9 0.0 copy-start.1
  14.9 0.5 shard_map.86
  15.5 0.0 copy-done.4
  15.5 0.0 copy-done.5
  15.5 3.4 %all-to-all-done = bf16[16,4,8,128]{3,2,1,0:T(8,128)(2,1)S(1)} async-done(((bf16[16,4,8,128]{3,2,1,0:T(8,128)(2,1)}), bf16[16,4,8,128]{3,2,1,0:T(8,128)(2,1)S(1)}, u32[]{:S(2)}, u32[]{:S(2)}) %all-to-all-start) | async-done | bytes 131104 | tf_op jit(solution)/shard_map/all_to_all | solution.py:78
  19.0 0.0 copy-done.1
  19.0 1.7 %shard_map.87 = f32[128,8,128]{2,1,0:T(8,128)S(1)} custom-call(s32[128]{0:T(128)S(1)} %compare_select_fusion.3.table_ref, bf16[48,256,128]{2,1,0:T(8,128)(2,1)S(1)} %bitcast.22, f32[8,128]{1,0:T(8,128)S(1)} %get-tuple-element.4.lines_ref, bf16[64,8,128]{2,1,0:T(8,128)(2,1)S(1)} %bitcast.24), custom_call_target="tpu_custom_call" | custom-call | flops 25165824 | bytes 4194304 | tf_op jit(solution)/shard_map/pallas_call | solution.py:121
  20.7 4.3 %collective-permute-start = (f32[64,8,128]{2,1,0:T(8,128)S(1)}, f32[64,8,128]{2,1,0:T(8,128)S(1)}, u32[]{:S(2)}, u32[]{:S(2)}) collective-permute-start(f32[64,8,128]{2,1,0:T(8,128)S(1)} %slice.17), channel_id=1, source_target_pairs={{0,1},{1,0},{2,3},{3,2},{4,5},{5,4},{6,7},{7,6},{8,9},{9,8},{10,11... | collective-permute-start | bytes 786440 | tf_op jit(solution)/shard_map/ppermute | solution.py:73
  25.0 1.1 %collective-permute-done = f32[64,8,128]{2,1,0:T(8,128)S(1)} collective-permute-done((f32[64,8,128]{2,1,0:T(8,128)S(1)}, f32[64,8,128]{2,1,0:T(8,128)S(1)}, u32[]{:S(2)}, u32[]{:S(2)}) %collective-permute-start) | collective-permute-done | bytes 262176 | tf_op jit(solution)/shard_map/ppermute | solution.py:73
  26.2 9.3 %all_to_all.25 = f32[4,16,8,128]{3,2,1,0:T(8,128)S(1)} all-to-all(f32[4,16,8,128]{3,2,1,0:T(8,128)S(1)} %bitcast.26), channel_id=1, replica_groups=mesh['zl'=4,'x'=4,'y'=4,'zh'=4,'c'=2] {'y'}, dimensions={0} | all-to-all | bytes 524288 | tf_op jit(solution)/shard_map/all_to_all | solution.py:84
  35.5 28.9 %all_to_all.26 = f32[4,17,8,128]{3,2,1,0:T(8,128)S(1)} all-to-all(f32[4,17,8,128]{3,2,1,0:T(8,128)S(1)} %broadcast_in_dim.37), channel_id=1, replica_groups=mesh['zl'=4,'x'=4,'y'=4,'zh'=4,'c'=2] {'zh'}, dimensions={0} | all-to-all | bytes 557056 | tf_op jit(solution)/shard_map/all_to_all | solution.py:78
  64.5 7.2 %all_to_all.27 = bf16[4,16,8,128]{3,2,1,0:T(8,128)(2,1)S(1)} all-to-all(bf16[4,16,8,128]{3,2,1,0:T(8,128)(2,1)S(1)} %broadcast_in_dim.38), channel_id=1, replica_groups=mesh['zl'=4,'x'=4,'y'=4,'zh'=4,'c'=2] {'y'}, dimensions={0} | all-to-all | bytes 262144 | tf_op jit(solution)/shard_map/all_to_all | solution.py:78
  71.7 7.3 %collective-permute-start.1 = (bf16[64,8,128]{2,1,0:T(8,128)(2,1)S(1)}, bf16[64,8,128]{2,1,0:T(8,128)(2,1)S(1)}, u32[]{:S(2)}, u32[]{:S(2)}) collective-permute-start(bf16[64,8,128]{2,1,0:T(8,128)(2,1)S(1)} %bitcast.27), channel_id=1, source_target_pairs={{0,1},{1,0},{2,3},{3,2},{4,5},{5,4},{6,7},{7,6},{8,9},{9,8},{10,11... | collective-permute-start | bytes 393224 | tf_op jit(solution)/shard_map/ppermute | solution.py:73
  79.0 1.0 collective-permute-done.1
  80.0 1.9 %shard_map.88 = f32[64,8,128]{2,1,0:T(8,128)} custom-call(s32[128]{0:T(128)S(1)} %compare_select_fusion.3.table_ref, bf16[48,256,128]{2,1,0:T(8,128)(2,1)S(1)} %bitcast.23, bf16[128,8,128]{2,1,0:T(8,128)(2,1)S(1)} %pad_maximum_fusion.scaled_ref), custom_call_target="tpu_custom_call" | custom-call | flops 25165824 | bytes 4194304 | tf_op jit(solution)/shard_map/pallas_call | solution.py:138
  81.9 5.8 %all-to-all-start.4 = ((f32[16,4,8,128]{3,2,1,0:T(8,128)}), f32[16,4,8,128]{3,2,1,0:T(8,128)S(1)}, u32[]{:S(2)}, u32[]{:S(2)}) async-start(f32[16,4,8,128]{3,2,1,0:T(8,128)} %bitcast.13), calls=%async_computation.4 | async-start | bytes 524288 | tf_op jit(solution)/shard_map/all_to_all | solution.py:84
  87.7 0.6 dynamic-slice_bitcast_fusion
  88.3 9.3 %all-to-all-done.4 = f32[16,4,8,128]{3,2,1,0:T(8,128)S(1)} async-done(((f32[16,4,8,128]{3,2,1,0:T(8,128)}), f32[16,4,8,128]{3,2,1,0:T(8,128)S(1)}, u32[]{:S(2)}, u32[]{:S(2)}) %all-to-all-start.4) | async-done | bytes 262176 | tf_op jit(solution)/shard_map/all_to_all | solution.py:84
  97.6 0.6 reduce_sum.29
  (11 shorter events, 0.2 us)
Async XLA Ops:
  0.6 14.9 %copy-start.4 = (s32[1,1,96]{2,1,0:T(1,128)S(1)}, s32[1,1,96]{2,1,0:T(1,128)}, u32[]{:S(2)}) copy-start(s32[1,1,96]{2,1,0:T(1,128)} %param.12) | copy-start | bytes 1156
  0.6 14.9 %copy-start.5 = (s32[1,1,96]{2,1,0:T(1,128)S(1)}, s32[1,1,96]{2,1,0:T(1,128)}, u32[]{:S(2)}) copy-start(s32[1,1,96]{2,1,0:T(1,128)} %param.11) | copy-start | bytes 1156
  2.0 16.9 %all-to-all-start = ((bf16[16,4,8,128]{3,2,1,0:T(8,128)(2,1)}), bf16[16,4,8,128]{3,2,1,0:T(8,128)(2,1)S(1)}, u32[]{:S(2)}, u32[]{:S(2)}) async-start(bf16[16,4,8,128]{3,2,1,0:T(8,128)(2,1)} %broadcast_in_dim.36), calls=%async_computation | async-start | bytes 262144 | tf_op jit(solution)/shard_map/all_to_all | solution.py:78
  11.7 1.9 %copy-start = (bf16[1,1,96,128,128]{4,3,2,1,0:T(8,128)(2,1)S(1)}, bf16[1,1,96,128,128]{4,3,2,1,0:T(8,128)(2,1)}, u32[]{:S(2)}) copy-start(bf16[1,1,96,128,128]{4,3,2,1,0:T(8,128)(2,1)} %param.10) | copy-start | bytes 9437188
  13.6 0.7 copy-start.2
  14.3 0.7 copy-start.3
  14.9 4.0 %copy-start.1 = (bf16[1,1,96,128,128]{4,3,2,1,0:T(8,128)(2,1)S(1)}, bf16[1,1,96,128,128]{4,3,2,1,0:T(8,128)(2,1)}, u32[]{:S(2)}) copy-start(bf16[1,1,96,128,128]{4,3,2,1,0:T(8,128)(2,1)} %param.10) | copy-start | bytes 9437188
  20.7 5.5 %collective-permute-start = (f32[64,8,128]{2,1,0:T(8,128)S(1)}, f32[64,8,128]{2,1,0:T(8,128)S(1)}, u32[]{:S(2)}, u32[]{:S(2)}) collective-permute-start(f32[64,8,128]{2,1,0:T(8,128)S(1)} %slice.17), channel_id=1, source_target_pairs={{0,1},{1,0},{2,3},{3,2},{4,5},{5,4},{6,7},{7,6},{8,9},{9,8},{10,11... | collective-permute-start | bytes 786440 | tf_op jit(solution)/shard_map/ppermute | solution.py:73
  71.7 8.3 %collective-permute-start.1 = (bf16[64,8,128]{2,1,0:T(8,128)(2,1)S(1)}, bf16[64,8,128]{2,1,0:T(8,128)(2,1)S(1)}, u32[]{:S(2)}, u32[]{:S(2)}) collective-permute-start(bf16[64,8,128]{2,1,0:T(8,128)(2,1)S(1)} %bitcast.27), channel_id=1, source_target_pairs={{0,1},{1,0},{2,3},{3,2},{4,5},{5,4},{6,7},{7,6},{8,9},{9,8},{10,11... | collective-permute-start | bytes 393224 | tf_op jit(solution)/shard_map/ppermute | solution.py:73
  81.9 15.7 %all-to-all-start.4 = ((f32[16,4,8,128]{3,2,1,0:T(8,128)}), f32[16,4,8,128]{3,2,1,0:T(8,128)S(1)}, u32[]{:S(2)}, u32[]{:S(2)}) async-start(f32[16,4,8,128]{3,2,1,0:T(8,128)} %bitcast.13), calls=%async_computation.4 | async-start | bytes 524288 | tf_op jit(solution)/shard_map/all_to_all | solution.py:84

commit v3 on v2

--- a/solution.py
+++ b/solution.py
@@ -17,14 +17,12 @@
     return ((c ^ core) << 4) | (y << 2) | zh
 
 
-def prepare(tiles_ref, theta_ref, diag_ref, lines_ref, block_ref):
+def prepare(theta_ref, lines_ref):
     line = lax.broadcasted_iota(jnp.int32, lines_ref.shape, 0)
     lines = jnp.zeros(lines_ref.shape, jnp.float32)
     for n in range(8):
         lines = jnp.where(line == n, theta_ref[n], lines)
     lines_ref[...] = lines
-    block_ref[0, :4] = diag_ref[...]
-    block_ref[0, 4:] = jnp.zeros((4, 128), jnp.float32)
 
 
 def forward(table_ref, tiles_ref, lines_ref, x_ref, out_ref, total):
@@ -56,9 +54,10 @@
 
 def backward(table_ref, tiles_ref, scaled_ref, out_ref, total):
     total[...] = jnp.zeros_like(total)
+    half = table_ref[AT_CORE] << 6
     for i in range(48):
         v, w = table_ref[2 * i], table_ref[2 * i + 1]
-        a, b = scaled_ref[(v >> 8) & 127], scaled_ref[(w >> 8) & 127]
+        a, b = scaled_ref[((v >> 8) & 127) ^ half], scaled_ref[((w >> 8) & 127) ^ half]
         none = jnp.zeros_like(a)
         both = jnp.concatenate(
             [jnp.concatenate([a, none], axis=0), jnp.concatenate([none, b], axis=0)], axis=1
@@ -67,10 +66,6 @@
         total[v & 255] = total[v & 255] + part[:8]
         total[w & 255] = total[w & 255] + part[8:]
     out_ref[...] = total[:64].astype(out_ref.dtype)
-
-
-def swap_cores(value):
-    return lax.ppermute(value, "c", [(0, 1), (1, 0)])
 
 
 def to_all(own, axes):
@@ -107,14 +102,14 @@
     f32 = functools.partial(jax.ShapeDtypeStruct, dtype=jnp.float32)
 
     tiles_here = tiles.reshape(slots // 2, 2 * width, width)
-    lines, diag_block = pl.pallas_call(
+    lines = pl.pallas_call(
         prepare,
-        out_shape=(f32((8, width)), f32((1, 8, width))),
-        in_specs=[vmem, smem, vmem],
-        out_specs=(vmem, vmem),
+        out_shape=f32((8, width)),
+        in_specs=[smem],
+        out_specs=vmem,
         compiler_params=params,
-        cost_estimate=cost,
-    )(tiles_here, theta, diag_rows.reshape(4, width))
+        cost_estimate=pl.CostEstimate(flops=1 << 31, bytes_accessed=8 << 20, transcendentals=0),
+    )(theta)
 
     own = x_cols.reshape(8, 4, width).transpose(1, 0, 2)
     x_all = to_all(own, ROW).reshape(64, 8, width)
@@ -128,12 +123,15 @@
         cost_estimate=cost,
     )(table, tiles_here, lines, x_all)
 
-    partial = sum_shares(partial[:64] + swap_cores(partial[64:]), "y")
-    got = to_all(jnp.concatenate([partial, diag_block], axis=0), "zh")
+    halves = lax.all_gather(partial[64:], "c")
+    partial = partial[:64] + lax.dynamic_index_in_dim(halves, 1 - core, 0, keepdims=False)
+    partial = sum_shares(partial, "y")
+    diag_block = jnp.pad(diag_rows.reshape(1, 4, width), ((0, 0), (0, 4), (0, 0)))
+    got = lax.all_gather(jnp.concatenate([partial, diag_block], axis=0), "zh")
     resid = jnp.sum(got[:, :16], axis=0)
     diag = got[:, 16, :4].reshape(16, 1, width)
     scaled = to_all((resid / diag).astype(jnp.bfloat16), "y").reshape(64, 8, width)
-    scaled = jnp.concatenate([scaled, swap_cores(scaled)], axis=0)
+    scaled = lax.all_gather(scaled, "c", tiled=True)
 
     back = pl.pallas_call(
         backward,

time: 98.8 us -> 88.6 us (0.90)
  starting transfers between devices: 26.4 us -> 12.5 us
  blocking collectives: 45.4 us -> 51.2 us
  local copies, waits for them, and re-layouts: 5.28 us -> 2.66 us
    all_gather x0 -> x3, blocking collectives: none -> 34.7 us  [the longest x1 22.3 us: body(): got = lax.all_gather(jnp.concatenate([partial, diag_block], axis=0), 'zh')]
    all_to_all x2 -> x1, blocking collectives: 36.1 us -> 7.21 us  [to_all(): return lax.all_to_all(copies, axes, 0, 0)]
    ppermute x2 -> x0, starting transfers between devices: 11.6 us -> none  [swap_cores(): return lax.ppermute(value, 'c', [(0, 1), (1, 0)])]
    unnamed x12 -> x6, local copies, waits for them, and re-layouts: 3.23 us -> 0.66 us
    all_to_all x1, starting transfers between devices: 5.79 us -> 3.53 us  [sum_shares(): lax.all_to_all(parts, axes, 0, 0).astype(jnp.float32)]
    ppermute x2 -> x0, waiting for transfers between devices: 2.1 us -> none  [swap_cores(): return lax.ppermute(value, 'c', [(0, 1), (1, 0)])]
    all_to_all x1, waiting for transfers between devices: 3.41 us -> 5.34 us  [to_all(): return lax.all_to_all(copies, axes, 0, 0)]
  transfers between devices with their start and end apart: 4 -> 2, of which waited for: 4 -> 2; matrix products, arithmetic and copies ran while one was open for 1% -> 1% of each run, Pallas kernels for 1% -> 1%
where the time goes in v3:
time: 88.6 us; the launch traced here: 88.1 us
  blocking collectives  51.2 us (58%)
  waiting for transfers between devices  14.8 us (17%)
  starting transfers between devices  12.5 us (14%)
  Pallas kernels  4.16 us (5%)
  local copies, waits for them, and re-layouts  2.66 us (3%)
  other arithmetic  1.41 us (2%)
  between operations  1.39 us (2%)
    all_gather x1, blocking collectives, body(): got = lax.all_gather(jnp.concatenate([partial, diag_block], axis=0), 'zh')  22.3 us
    all_to_all x1, waiting for transfers between devices, sum_shares(): lax.all_to_all(parts, axes, 0, 0).astype(jnp.float32)  9.48 us
    all_to_all x1, blocking collectives, sum_shares(): lax.all_to_all(parts, axes, 0, 0).astype(jnp.float32)  9.28 us
    all_to_all x1, starting transfers between devices, to_all(): return lax.all_to_all(copies, axes, 0, 0)  9.01 us
    all_gather x1, blocking collectives, body(): scaled = lax.all_gather(scaled, 'c', tiled=True)  8.17 us
    all_to_all x1, blocking collectives, to_all(): return lax.all_to_all(copies, axes, 0, 0)  7.21 us
    all_to_all x1, waiting for transfers between devices, to_all(): return lax.all_to_all(copies, axes, 0, 0)  5.34 us
    all_gather x1, blocking collectives, body(): halves = lax.all_gather(partial[64:], 'c')  4.18 us
  transfers between devices with their start and end apart: 2, of which 2 were waited for; matrix products, arithmetic and copies ran while one was open for 1% of the time, Pallas kernels for 1%

profile of v3, /device:TPU:1, one launch (start us, length us, event | category | flops | bytes accessed | tf_op | source)
XLA Modules:
  0.0 88.1 jit_solution(5121031111909929588)
XLA Ops:
  0.6 1.4 %broadcast_in_dim.30 = bf16[16,4,8,128]{3,2,1,0:T(8,128)(2,1)} broadcast(bf16[4,8,128]{2,1,0:T(8,128)(2,1)} %bitcast.35), dimensions={1,2,3} | broadcast | bytes 139264 | tf_op jit(solution)/shard_map/broadcast_in_dim | solution.py:72
  2.0 9.0 %all-to-all-start = ((bf16[16,4,8,128]{3,2,1,0:T(8,128)(2,1)}), bf16[16,4,8,128]{3,2,1,0:T(8,128)(2,1)S(1)}, u32[]{:S(2)}, u32[]{:S(2)}) async-start(bf16[16,4,8,128]{3,2,1,0:T(8,128)(2,1)} %broadcast_in_dim.30), calls=%async_computation | async-start | bytes 262144 | tf_op jit(solution)/shard_map/all_to_all | solution.py:73
  11.7 0.7 compare_select_fusion.3.table_ref
  12.4 0.0 copy-start.1
  12.4 0.6 copy-done.1
  13.0 0.0 copy-start
  13.0 0.5 shard_map.86.lines_ref
  13.6 5.3 %all-to-all-done = bf16[16,4,8,128]{3,2,1,0:T(8,128)(2,1)S(1)} async-done(((bf16[16,4,8,128]{3,2,1,0:T(8,128)(2,1)}), bf16[16,4,8,128]{3,2,1,0:T(8,128)(2,1)S(1)}, u32[]{:S(2)}, u32[]{:S(2)}) %all-to-all-start) | async-done | bytes 131104 | tf_op jit(solution)/shard_map/all_to_all | solution.py:73
  18.9 0.0 copy-done
  18.9 0.0 copy-start.2
  18.9 1.7 %shard_map.87 = f32[128,8,128]{2,1,0:T(8,128)S(1)} custom-call(s32[128]{0:T(128)S(1)} %compare_select_fusion.3.table_ref, bf16[48,256,128]{2,1,0:T(8,128)(2,1)S(1)} %bitcast.25, f32[8,128]{1,0:T(8,128)S(1)} %shard_map.86.lines_ref, bf16[64,8,128]{2,1,0:T(8,128)(2,1)S(1)} %bitcast.27), custom_call_target="tpu_custom_call" | custom-call | flops 25165824 | bytes 4194304 | tf_op jit(solution)/shard_map/pallas_call | solution.py:116
  20.6 4.2 %all-gather = f32[128,8,128]{2,1,0:T(8,128)S(1)} all-gather(f32[64,8,128]{2,1,0:T(8,128)S(1)} %slice.17), channel_id=2, replica_groups=mesh['zl'=4,'x'=4,'y'=4,'zh'=4,'c'=2] {'c'}, dimensions={0}, use_global_device_ids=true | all-gather | bytes 786432 | tf_op jit(solution)/shard_map/all_gather | solution.py:126
  24.8 9.3 %all_to_all.20 = f32[4,16,8,128]{3,2,1,0:T(8,128)S(1)} all-to-all(f32[4,16,8,128]{3,2,1,0:T(8,128)S(1)} %bitcast.31), channel_id=1, replica_groups=mesh['zl'=4,'x'=4,'y'=4,'zh'=4,'c'=2] {'y'}, dimensions={0} | all-to-all | bytes 524288 | tf_op jit(solution)/shard_map/all_to_all | solution.py:79
  34.2 0.0 copy-done.2
  34.2 22.3 %all-gather.1 = f32[68,8,128]{2,1,0:T(8,128)S(1)} all-gather(f32[17,8,128]{2,1,0:T(8,128)S(1)} %select_maximum_fusion), channel_id=3, replica_groups=mesh['zl'=4,'x'=4,'y'=4,'zh'=4,'c'=2] {'zh'}, dimensions={0}, use_global_device_ids=true | all-gather | bytes 348160 | tf_op jit(solution)/shard_map/all_gather | solution.py:130
  56.6 7.2 %all_to_all.21 = bf16[4,16,8,128]{3,2,1,0:T(8,128)(2,1)S(1)} all-to-all(bf16[4,16,8,128]{3,2,1,0:T(8,128)(2,1)S(1)} %broadcast_in_dim.31), channel_id=1, replica_groups=mesh['zl'=4,'x'=4,'y'=4,'zh'=4,'c'=2] {'y'}, dimensions={0} | all-to-all | bytes 262144 | tf_op jit(solution)/shard_map/all_to_all | solution.py:73
  63.8 8.2 %all_gather.19.scaled_ref = bf16[128,8,128]{2,1,0:T(8,128)(2,1)S(1)} all-gather(bf16[64,8,128]{2,1,0:T(8,128)(2,1)S(1)} %bitcast.32), channel_id=1, replica_groups=mesh['zl'=4,'x'=4,'y'=4,'zh'=4,'c'=2] {'c'}, dimensions={0}, use_global_device_ids=true | all-gather | bytes 393216 | tf_op jit(solution)/shard_map/all_gather | solution.py:134
  71.9 1.9 %shard_map.88 = f32[64,8,128]{2,1,0:T(8,128)} custom-call(s32[128]{0:T(128)S(1)} %compare_select_fusion.3.table_ref, bf16[48,256,128]{2,1,0:T(8,128)(2,1)S(1)} %bitcast.26, bf16[128,8,128]{2,1,0:T(8,128)(2,1)S(1)} %all_gather.19.scaled_ref), custom_call_target="tpu_custom_call" | custom-call | flops 25165824 | bytes 4194304 | tf_op jit(solution)/shard_map/pallas_call | solution.py:136
  73.9 3.5 %all-to-all-start.3 = ((f32[16,4,8,128]{3,2,1,0:T(8,128)}), f32[16,4,8,128]{3,2,1,0:T(8,128)S(1)}, u32[]{:S(2)}, u32[]{:S(2)}) async-start(f32[16,4,8,128]{3,2,1,0:T(8,128)} %bitcast.16), calls=%async_computation.3 | async-start | bytes 524288 | tf_op jit(solution)/shard_map/all_to_all | solution.py:79
  77.4 0.6 dynamic-slice_bitcast_fusion
  78.0 9.5 %all-to-all-done.3 = f32[16,4,8,128]{3,2,1,0:T(8,128)S(1)} async-done(((f32[16,4,8,128]{3,2,1,0:T(8,128)}), f32[16,4,8,128]{3,2,1,0:T(8,128)S(1)}, u32[]{:S(2)}, u32[]{:S(2)}) %all-to-all-start.3) | async-done | bytes 262176 | tf_op jit(solution)/shard_map/all_to_all | solution.py:79
  87.5 0.6 reduce_sum.29
  (8 shorter events, 0.1 us)
Async XLA Ops:
  2.0 16.9 %all-to-all-start = ((bf16[16,4,8,128]{3,2,1,0:T(8,128)(2,1)}), bf16[16,4,8,128]{3,2,1,0:T(8,128)(2,1)S(1)}, u32[]{:S(2)}, u32[]{:S(2)}) async-start(bf16[16,4,8,128]{3,2,1,0:T(8,128)(2,1)} %broadcast_in_dim.30), calls=%async_computation | async-start | bytes 262144 | tf_op jit(solution)/shard_map/all_to_all | solution.py:73
  12.4 0.7 copy-start.1
  13.0 5.9 %copy-start = (bf16[1,1,96,128,128]{4,3,2,1,0:T(8,128)(2,1)S(1)}, bf16[1,1,96,128,128]{4,3,2,1,0:T(8,128)(2,1)}, u32[]{:S(2)}) copy-start(bf16[1,1,96,128,128]{4,3,2,1,0:T(8,128)(2,1)} %param.10) | copy-start | bytes 9437188
  18.9 15.2 %copy-start.2 = (f32[512]{0:T(512)S(1)}, f32[512]{0:T(512)}, u32[]{:S(2)}) copy-start(f32[512]{0:T(512)} %param.8) | copy-start | bytes 6148
  73.9 13.6 %all-to-all-start.3 = ((f32[16,4,8,128]{3,2,1,0:T(8,128)}), f32[16,4,8,128]{3,2,1,0:T(8,128)S(1)}, u32[]{:S(2)}, u32[]{:S(2)}) async-start(f32[16,4,8,128]{3,2,1,0:T(8,128)} %bitcast.16), calls=%async_computation.3 | async-start | bytes 524288 | tf_op jit(solution)/shard_map/all_to_all | solution.py:79

commit v4 on v3

--- a/solution.py
+++ b/solution.py
@@ -17,12 +17,14 @@
     return ((c ^ core) << 4) | (y << 2) | zh
 
 
-def prepare(theta_ref, lines_ref):
+def prepare(theta_ref, diag_ref, lines_ref, block_ref):
     line = lax.broadcasted_iota(jnp.int32, lines_ref.shape, 0)
     lines = jnp.zeros(lines_ref.shape, jnp.float32)
     for n in range(8):
         lines = jnp.where(line == n, theta_ref[n], lines)
     lines_ref[...] = lines
+    block_ref[:4] = diag_ref[...]
+    block_ref[4:] = jnp.zeros((4, 128), jnp.float32)
 
 
 def forward(table_ref, tiles_ref, lines_ref, x_ref, out_ref, total):
@@ -79,6 +81,11 @@
     return jnp.sum(lax.all_to_all(parts, axes, 0, 0).astype(jnp.float32), axis=0)
 
 
+def gather_pairs(partial, diag, pairs):
+    block = jnp.concatenate([partial, diag[None]], axis=0)
+    return lax.all_gather(block, "zh", axis_index_groups=pairs)
+
+
 def vectors_of(blocks):
     return blocks.transpose(1, 0, 2).reshape(blocks.shape[1], -1)
 
@@ -102,14 +109,14 @@
     f32 = functools.partial(jax.ShapeDtypeStruct, dtype=jnp.float32)
 
     tiles_here = tiles.reshape(slots // 2, 2 * width, width)
-    lines = pl.pallas_call(
+    lines, diag = pl.pallas_call(
         prepare,
-        out_shape=f32((8, width)),
-        in_specs=[smem],
-        out_specs=vmem,
+        out_shape=(f32((8, width)), f32((8, width))),
+        in_specs=[smem, vmem],
+        out_specs=(vmem, vmem),
         compiler_params=params,
         cost_estimate=pl.CostEstimate(flops=1 << 31, bytes_accessed=8 << 20, transcendentals=0),
-    )(theta)
+    )(theta, diag_rows.reshape(4, width))
 
     own = x_cols.reshape(8, 4, width).transpose(1, 0, 2)
     x_all = to_all(own, ROW).reshape(64, 8, width)
@@ -126,10 +133,11 @@
     halves = lax.all_gather(partial[64:], "c")
     partial = partial[:64] + lax.dynamic_index_in_dim(halves, 1 - core, 0, keepdims=False)
     partial = sum_shares(partial, "y")
-    diag_block = jnp.pad(diag_rows.reshape(1, 4, width), ((0, 0), (0, 4), (0, 0)))
-    got = lax.all_gather(jnp.concatenate([partial, diag_block], axis=0), "zh")
-    resid = jnp.sum(got[:, :16], axis=0)
-    diag = got[:, 16, :4].reshape(16, 1, width)
+    got = gather_pairs(partial, diag, [[0, 1], [2, 3]])
+    diag = got[:, 16, :4].reshape(8, width)
+    got = gather_pairs(got[0, :16] + got[1, :16], diag, [[0, 3], [1, 2]])
+    resid = got[0, :16] + got[1, :16]
+    diag = got[:, 16].reshape(16, 1, width)
     scaled = to_all((resid / diag).astype(jnp.bfloat16), "y").reshape(64, 8, width)
     scaled = lax.all_gather(scaled, "c", tiled=True)
 

time: 88.6 us -> 87 us (0.982)
  blocking collectives: 51.2 us -> 46.9 us
  starting transfers between devices: 12.5 us -> 15.4 us
    all_gather x1, blocking collectives: 8.17 us -> 4.26 us  [body(): scaled = lax.all_gather(scaled, 'c', tiled=True)]
    all_to_all x1, starting transfers between devices: 3.53 us -> 6.36 us  [sum_shares(): lax.all_to_all(parts, axes, 0, 0).astype(jnp.float32)]
    all_gather x1 -> x2, blocking collectives: 22.3 us -> 21.9 us  [gather_pairs(): return lax.all_gather(block, 'zh', axis_index_groups=pairs)]
  transfers between devices with their start and end apart: 2 -> 2, of which waited for: 2 -> 2; matrix products, arithmetic and copies ran while one was open for 1% -> 2% of each run, Pallas kernels for 1% -> 1%
where the time goes in v4:
time: 87 us; the launch traced here: 86.5 us
  blocking collectives  46.9 us (54%)
  starting transfers between devices  15.4 us (18%)
  waiting for transfers between devices  14 us (16%)
  Pallas kernels  4.17 us (5%)
  local copies, waits for them, and re-layouts  3.34 us (4%)
  other arithmetic  1.41 us (2%)
  between operations  1.39 us (2%)
    all_gather x2, blocking collectives, gather_pairs(): return lax.all_gather(block, 'zh', axis_index_groups=pairs)  21.9 us
    all_to_all x1, waiting for transfers between devices, sum_shares(): lax.all_to_all(parts, axes, 0, 0).astype(jnp.float32)  9.3 us
    all_to_all x1, blocking collectives, sum_shares(): lax.all_to_all(parts, axes, 0, 0).astype(jnp.float32)  9.26 us
    all_to_all x1, starting transfers between devices, to_all(): return lax.all_to_all(copies, axes, 0, 0)  9.01 us
    all_to_all x1, blocking collectives, to_all(): return lax.all_to_all(copies, axes, 0, 0)  7.21 us
    all_to_all x1, starting transfers between devices, sum_shares(): lax.all_to_all(parts, axes, 0, 0).astype(jnp.float32)  6.36 us
    all_to_all x1, waiting for transfers between devices, to_all(): return lax.all_to_all(copies, axes, 0, 0)  4.65 us
    all_gather x1, blocking collectives, body(): scaled = lax.all_gather(scaled, 'c', tiled=True)  4.26 us
  transfers between devices with their start and end apart: 2, of which 2 were waited for; matrix products, arithmetic and copies ran while one was open for 2% of the time, Pallas kernels for 1%

profile of v4, /device:TPU:1, one launch (start us, length us, event | category | flops | bytes accessed | tf_op | source)
XLA Modules:
  0.0 86.5 jit_solution(3148718307619564281)
XLA Ops:
  0.6 1.4 %broadcast_in_dim.35 = bf16[16,4,8,128]{3,2,1,0:T(8,128)(2,1)} broadcast(bf16[4,8,128]{2,1,0:T(8,128)(2,1)} %bitcast.49), dimensions={1,2,3} | broadcast | bytes 139264 | tf_op jit(solution)/shard_map/broadcast_in_dim | solution.py:74
  2.0 9.0 %all-to-all-start = ((bf16[16,4,8,128]{3,2,1,0:T(8,128)(2,1)}), bf16[16,4,8,128]{3,2,1,0:T(8,128)(2,1)S(1)}, u32[]{:S(2)}, u32[]{:S(2)}) async-start(bf16[16,4,8,128]{3,2,1,0:T(8,128)(2,1)} %broadcast_in_dim.35), calls=%async_computation | async-start | bytes 262144 | tf_op jit(solution)/shard_map/all_to_all | solution.py:75
  11.7 0.7 compare_select_fusion.3.table_ref
  12.4 0.0 copy-start.1
  12.4 0.7 copy-done.1
  13.0 0.0 copy-start.2
  13.0 0.7 copy-done.2
  13.7 0.0 copy-start
  13.7 0.5 shard_map.86
  14.3 4.7 %all-to-all-done = bf16[16,4,8,128]{3,2,1,0:T(8,128)(2,1)S(1)} async-done(((bf16[16,4,8,128]{3,2,1,0:T(8,128)(2,1)}), bf16[16,4,8,128]{3,2,1,0:T(8,128)(2,1)S(1)}, u32[]{:S(2)}, u32[]{:S(2)}) %all-to-all-start) | async-done | bytes 131104 | tf_op jit(solution)/shard_map/all_to_all | solution.py:75
  18.9 0.0 copy-done
  18.9 1.7 %shard_map.87 = f32[128,8,128]{2,1,0:T(8,128)S(1)} custom-call(s32[128]{0:T(128)S(1)} %compare_select_fusion.3.table_ref, bf16[48,256,128]{2,1,0:T(8,128)(2,1)S(1)} %bitcast.35, f32[8,128]{1,0:T(8,128)S(1)} %get-tuple-element.4.lines_ref, bf16[64,8,128]{2,1,0:T(8,128)(2,1)S(1)} %bitcast.37), custom_call_target="tpu_custom_call" | custom-call | flops 25165824 | bytes 4194304 | tf_op jit(solution)/shard_map/pallas_call | solution.py:123
  20.6 4.2 %all-gather = f32[128,8,128]{2,1,0:T(8,128)S(1)} all-gather(f32[64,8,128]{2,1,0:T(8,128)S(1)} %slice.33), channel_id=2, replica_groups=mesh['zl'=4,'x'=4,'y'=4,'zh'=4,'c'=2] {'c'}, dimensions={0}, use_global_device_ids=true | all-gather | bytes 786432 | tf_op jit(solution)/shard_map/all_gather | solution.py:133
  24.9 9.3 %all_to_all.20 = f32[4,16,8,128]{3,2,1,0:T(8,128)S(1)} all-to-all(f32[4,16,8,128]{3,2,1,0:T(8,128)S(1)} %bitcast.41), channel_id=1, replica_groups=mesh['zl'=4,'x'=4,'y'=4,'zh'=4,'c'=2] {'y'}, dimensions={0} | all-to-all | bytes 524288 | tf_op jit(solution)/shard_map/all_to_all | solution.py:81
  34.2 14.0 %all-gather.1 = f32[34,8,128]{2,1,0:T(8,128)S(1)} all-gather(f32[17,8,128]{2,1,0:T(8,128)S(1)} %pad_maximum_fusion), channel_id=3, replica_groups={{0,2},{4,6},{1,3},{5,7},{8,10},{12,14},{9,11},{13,15},{16,18},{20,22},{..., dimensions={0}, use_global_device_ids=true | all-gather | bytes 208896 | tf_op jit(solution)/shard_map/all_gather | solution.py:86
  48.2 7.9 %all-gather.2 = f32[34,8,128]{2,1,0:T(8,128)S(1)} all-gather(f32[17,8,128]{2,1,0:T(8,128)S(1)} %pad_maximum_fusion.1), channel_id=4, replica_groups={{0,6},{2,4},{1,7},{3,5},{8,14},{10,12},{9,15},{11,13},{16,22},{18,20},{..., dimensions={0}, use_global_device_ids=true | all-gather | bytes 208896 | tf_op jit(solution)/shard_map/all_gather | solution.py:86
  56.2 7.2 %all_to_all.21 = bf16[4,16,8,128]{3,2,1,0:T(8,128)(2,1)S(1)} all-to-all(bf16[4,16,8,128]{3,2,1,0:T(8,128)(2,1)S(1)} %broadcast_in_dim.38), channel_id=1, replica_groups=mesh['zl'=4,'x'=4,'y'=4,'zh'=4,'c'=2] {'y'}, dimensions={0} | all-to-all | bytes 262144 | tf_op jit(solution)/shard_map/all_to_all | solution.py:75
  63.4 4.3 %all_gather.27.scaled_ref = bf16[128,8,128]{2,1,0:T(8,128)(2,1)S(1)} all-gather(bf16[64,8,128]{2,1,0:T(8,128)(2,1)S(1)} %bitcast.46), channel_id=1, replica_groups=mesh['zl'=4,'x'=4,'y'=4,'zh'=4,'c'=2] {'c'}, dimensions={0}, use_global_device_ids=true | all-gather | bytes 393216 | tf_op jit(solution)/shard_map/all_gather | solution.py:142
  67.7 1.9 %shard_map.88 = f32[64,8,128]{2,1,0:T(8,128)} custom-call(s32[128]{0:T(128)S(1)} %compare_select_fusion.3.table_ref, bf16[48,256,128]{2,1,0:T(8,128)(2,1)S(1)} %bitcast.36, bf16[128,8,128]{2,1,0:T(8,128)(2,1)S(1)} %all_gather.27.scaled_ref), custom_call_target="tpu_custom_call" | custom-call | flops 25165824 | bytes 4194304 | tf_op jit(solution)/shard_map/pallas_call | solution.py:144
  69.6 6.4 %all-to-all-start.3 = ((f32[16,4,8,128]{3,2,1,0:T(8,128)}), f32[16,4,8,128]{3,2,1,0:T(8,128)S(1)}, u32[]{:S(2)}, u32[]{:S(2)}) async-start(f32[16,4,8,128]{3,2,1,0:T(8,128)} %bitcast.22), calls=%async_computation.3 | async-start | bytes 524288 | tf_op jit(solution)/shard_map/all_to_all | solution.py:81
  76.0 0.6 dynamic-slice_bitcast_fusion
  76.6 9.3 %all-to-all-done.3 = f32[16,4,8,128]{3,2,1,0:T(8,128)S(1)} async-done(((f32[16,4,8,128]{3,2,1,0:T(8,128)}), f32[16,4,8,128]{3,2,1,0:T(8,128)S(1)}, u32[]{:S(2)}, u32[]{:S(2)}) %all-to-all-start.3) | async-done | bytes 262176 | tf_op jit(solution)/shard_map/all_to_all | solution.py:81
  85.9 0.6 reduce_sum.19
  (10 shorter events, 0.1 us)
Async XLA Ops:
  2.0 16.9 %all-to-all-start = ((bf16[16,4,8,128]{3,2,1,0:T(8,128)(2,1)}), bf16[16,4,8,128]{3,2,1,0:T(8,128)(2,1)S(1)}, u32[]{:S(2)}, u32[]{:S(2)}) async-start(bf16[16,4,8,128]{3,2,1,0:T(8,128)(2,1)} %broadcast_in_dim.35), calls=%async_computation | async-start | bytes 262144 | tf_op jit(solution)/shard_map/all_to_all | solution.py:75
  12.4 0.7 copy-start.1
  13.0 0.7 copy-start.2
  13.7 5.2 %copy-start = (bf16[1,1,96,128,128]{4,3,2,1,0:T(8,128)(2,1)S(1)}, bf16[1,1,96,128,128]{4,3,2,1,0:T(8,128)(2,1)}, u32[]{:S(2)}) copy-start(bf16[1,1,96,128,128]{4,3,2,1,0:T(8,128)(2,1)} %param.10) | copy-start | bytes 9437188
  69.6 16.3 %all-to-all-start.3 = ((f32[16,4,8,128]{3,2,1,0:T(8,128)}), f32[16,4,8,128]{3,2,1,0:T(8,128)S(1)}, u32[]{:S(2)}, u32[]{:S(2)}) async-start(f32[16,4,8,128]{3,2,1,0:T(8,128)} %bitcast.22), calls=%async_computation.3 | async-start | bytes 524288 | tf_op jit(solution)/shard_map/all_to_all | solution.py:81

commit v5 on v4

v5 whole, which is shorter than its diff:
```python
import functools

import jax
import jax.numpy as jnp
from jax import lax
from jax.experimental import pallas as pl
from jax.experimental.pallas import tpu as pltpu
from jax.sharding import Mesh, PartitionSpec as P

ROW = ("zl", "x")
COL = ("y", "zh", "c")
BACK = jnp.bfloat16
AT_ROW, AT_COL, AT_CORE, AT_ZH, AT_THETA = 96, 97, 98, 99, 104


def place(share, core):
    y, zh, c = share >> 3, (share >> 1) & 3, share & 1
    return ((c ^ core) << 4) | (y << 2) | zh


def settle(table_ref, out_ref):
    out_ref[...] = table_ref[...]


def number(table_ref, at):
    return table_ref[at].astype(jnp.int32)


def forward(table_ref, tiles_ref, x_ref, out_ref, total):
    total[...] = jnp.zeros_like(total)
    row, col = number(table_ref, AT_ROW), number(table_ref, AT_COL)

    @pl.when(row == col >> 1)
    def _():
        first = (col & 1) * 16
        line = lax.broadcasted_iota(jnp.int32, (8, 128), 0)
        theta = jnp.zeros((8, 128), jnp.float32)
        for n in range(8):
            theta = jnp.where(line == n, table_ref[AT_THETA + n], theta)

        def shift(s, carry):
            p = place(first + s, col & 1) * 4
            for j in range(4):
                total[p + j] = -theta * x_ref[s * 4 + j].astype(jnp.float32)
            return carry

        lax.fori_loop(0, 16, shift, 0)

    for i in range(48):
        v, w = number(table_ref, 2 * i), number(table_ref, 2 * i + 1)
        both = jnp.concatenate([x_ref[v & 63], x_ref[w & 63]], axis=0)
        part = lax.dot_general(
            both, tiles_ref[i], (((1,), (1,)), ((), ())), preferred_element_type=jnp.float32
        )
        total[v >> 8] = total[v >> 8] + part[:8, :128]
        total[w >> 8] = total[w >> 8] + part[8:, 128:]
    out_ref[...] = total[:128]


def backward(table_ref, tiles_ref, scaled_ref, resid_ref, out_ref, own_ref, total, sem):
    own = resid_ref.at[pl.ds(number(table_ref, AT_ZH) * 4, 4)]
    copy = pltpu.make_async_copy(own, own_ref, sem)
    copy.start()
    total[...] = jnp.zeros_like(total)
    half = number(table_ref, AT_CORE) << 6
    for i in range(48):
        v, w = number(table_ref, 2 * i), number(table_ref, 2 * i + 1)
        a, b = scaled_ref[((v >> 8) & 127) ^ half], scaled_ref[((w >> 8) & 127) ^ half]
        none = jnp.zeros_like(a)
        both = jnp.concatenate(
            [jnp.concatenate([a, none], axis=0), jnp.concatenate([none, b], axis=0)], axis=1
        )
        part = jnp.dot(both, tiles_ref[i], preferred_element_type=jnp.float32)
        total[v & 255] = total[v & 255] + part[:8]
        total[w & 255] = total[w & 255] + part[8:]
    out_ref[...] = total[:64].astype(out_ref.dtype)
    copy.wait()


def to_all(own, axes):
    copies = jnp.broadcast_to(own[None], (lax.axis_size(axes), *own.shape))
    return lax.all_to_all(copies, axes, 0, 0)


def sum_shares(parts, axes):
    n = lax.axis_size(axes)
    parts = parts.reshape(n, parts.shape[0] // n, *parts.shape[1:])
    return jnp.sum(lax.all_to_all(parts, axes, 0, 0).astype(jnp.float32), axis=0)


def gather_pairs(partial, diag, pairs):
    diag = jnp.pad(diag, ((0, 0), (0, 8 - diag.shape[1]), (0, 0)))
    return lax.all_gather(jnp.concatenate([partial, diag], axis=0), "zh", axis_index_groups=pairs)


def vectors_of(blocks):
    return blocks.transpose(1, 0, 2).reshape(blocks.shape[1], -1)


def body(x_cols, diag_rows, theta, tiles, tile_rows, tile_cols, counts):
    core = lax.axis_index("c")
    slots, width = tiles.shape[2], tiles.shape[3]
    rows = jnp.pad(tile_rows[0, 0], (0, 32))
    cols = jnp.pad(tile_cols[0, 0], (0, 32))
    slot = jnp.arange(slots + 32, dtype=jnp.int32)
    used = slot < counts[0, 0]
    table = jnp.where(used, ((place(rows >> 2, core) << 2) | (rows & 3)) << 8 | cols, 128 << 8 | 64)
    table = jnp.where(slot == AT_ROW, lax.axis_index(ROW), table)
    table = jnp.where(slot == AT_COL, lax.axis_index(COL), table)
    table = jnp.where(slot == AT_CORE, core, table)
    table = jnp.where(slot == AT_ZH, lax.axis_index("zh"), table).astype(jnp.float32)
    table = jnp.where(slot < AT_THETA, table, jnp.pad(theta, (AT_THETA, 16)))

    smem = pl.BlockSpec(memory_space=pltpu.SMEM)
    vmem = pl.BlockSpec(memory_space=pltpu.VMEM)
    params = pltpu.CompilerParams(vmem_limit_bytes=16 * 1024 * 1024)
    cost = pl.CostEstimate(flops=2 * slots * 8 * width * width, bytes_accessed=4 << 20, transcendentals=0)
    f32 = functools.partial(jax.ShapeDtypeStruct, dtype=jnp.float32)

    tiles_here = tiles.reshape(slots // 2, 2 * width, width)
    table = pl.pallas_call(
        settle,
        out_shape=f32(table.shape),
        in_specs=[vmem],
        out_specs=vmem,
        compiler_params=params,
        cost_estimate=pl.CostEstimate(flops=1 << 31, bytes_accessed=8 << 20, transcendentals=0),
    )(table)

    own = x_cols.reshape(8, 4, width).transpose(1, 0, 2)
    x_all = to_all(own, ROW).reshape(64, 8, width)
    partial = pl.pallas_call(
        forward,
        out_shape=f32((128, 8, width)),
        in_specs=[smem, vmem, vmem],
        out_specs=vmem,
        scratch_shapes=[pltpu.VMEM((136, 8, width), jnp.float32)],
        compiler_params=params,
        cost_estimate=cost,
    )(table, tiles_here, x_all)

    halves = lax.all_gather(partial[64:], "c")
    partial = partial[:64] + lax.dynamic_index_in_dim(halves, 1 - core, 0, keepdims=False)
    partial = sum_shares(partial, "y")
    got = gather_pairs(partial, diag_rows.reshape(1, 4, width), [[0, 1], [2, 3]])
    diag = got[:, 16, :4].reshape(1, 8, width)
    got = gather_pairs(got[0, :16] + got[1, :16], diag, [[0, 3], [1, 2]])
    resid = got[0, :16] + got[1, :16]
    diag = got[:, 16].reshape(16, 1, width)
    scaled = to_all((resid / diag).astype(jnp.bfloat16), "y").reshape(64, 8, width)
    scaled = lax.all_gather(scaled, "c", tiled=True)

    back, resid = pl.pallas_call(
        backward,
        out_shape=(jax.ShapeDtypeStruct((64, 8, width), BACK), f32((4, 8, width))),
        in_specs=[smem, vmem, vmem, vmem],
        out_specs=(vmem, pl.BlockSpec(memory_space=pl.ANY)),
        scratch_shapes=[pltpu.VMEM((72, 8, width), jnp.float32), pltpu.SemaphoreType.DMA],
        compiler_params=params,
        cost_estimate=cost,
    )(table, tiles_here, scaled, resid)
    return vectors_of(resid), vectors_of(sum_shares(back, ROW))


def solution(mesh):
    fine = Mesh(mesh.devices.reshape(4, 4, 4, 4, 2), ROW + COL)
    return jax.shard_map(
        body,
        mesh=fine,
        in_specs=(
            P(None, COL + ROW),
            P(ROW + COL),
            P(),
            P(ROW, COL, None, None, None),
            P(ROW, COL, None),
            P(ROW, COL, None),
            P(ROW, COL),
        ),
        out_specs=(P(None, ROW + COL), P(None, COL + ROW)),
        check_vma=False,
    )
```

time: 87 us -> 84.1 us (0.967)
  blocking collectives: 46.9 us -> 60.5 us
  waiting for transfers between devices: 14 us -> 6.47 us
  starting transfers between devices: 15.4 us -> 9.01 us
  local copies, waits for them, and re-layouts: 3.34 us -> 1.41 us
    all_to_all x1 -> x2, blocking collectives: 9.26 us -> 22.9 us  [sum_shares(): lax.all_to_all(parts, axes, 0, 0).astype(jnp.float32)]
    all_to_all x1 -> x0, waiting for transfers between devices: 9.3 us -> none  [sum_shares(): lax.all_to_all(parts, axes, 0, 0).astype(jnp.float32)]
    all_to_all x1 -> x0, starting transfers between devices: 6.36 us -> none  [sum_shares(): lax.all_to_all(parts, axes, 0, 0).astype(jnp.float32)]
    all_to_all x1, waiting for transfers between devices: 4.65 us -> 6.47 us  [to_all(): return lax.all_to_all(copies, axes, 0, 0)]
    unnamed x6 -> x4, local copies, waits for them, and re-layouts: 1.33 us -> 0.01 us
  transfers between devices with their start and end apart: 2 -> 1, of which waited for: 2 -> 1; matrix products, arithmetic and copies ran while one was open for 2% -> 1% of each run, Pallas kernels for 1% -> 0%
where the time goes in v5:
time: 84.1 us; the launch traced here: 83.7 us
  blocking collectives  60.5 us (72%)
  starting transfers between devices  9.01 us (11%)
  waiting for transfers between devices  6.47 us (8%)
  Pallas kernels  3.43 us (4%)
  other arithmetic  1.49 us (2%)
  local copies, waits for them, and re-layouts  1.41 us (2%)
  between operations  1.37 us (2%)
    all_to_all x2, blocking collectives, sum_shares(): lax.all_to_all(parts, axes, 0, 0).astype(jnp.float32)  22.9 us
    all_gather x2, blocking collectives, gather_pairs(): lax.all_gather(jnp.concatenate([partial, diag], axis=0), 'zh', axis_index...  21.9 us
    all_to_all x1, starting transfers between devices, to_all(): return lax.all_to_all(copies, axes, 0, 0)  9.01 us
    all_to_all x1, blocking collectives, to_all(): return lax.all_to_all(copies, axes, 0, 0)  7.21 us
    all_to_all x1, waiting for transfers between devices, to_all(): return lax.all_to_all(copies, axes, 0, 0)  6.47 us
    all_gather x1, blocking collectives, body(): scaled = lax.all_gather(scaled, 'c', tiled=True)  4.32 us
    all_gather x1, blocking collectives, body(): halves = lax.all_gather(partial[64:], 'c')  4.17 us
    pallas_call x1, Pallas kernels, body(): pl.pallas_call(backward, out_shape=(jax.ShapeDtypeStruct((64, 8, width),...  1.74 us
  transfers between devices with their start and end apart: 1, of which 1 were waited for; matrix products, arithmetic and copies ran while one was open for 1% of the time, Pallas kernels for 0%

profile of v5, /device:TPU:1, one launch (start us, length us, event | category | flops | bytes accessed | tf_op | source)
XLA Modules:
  0.0 83.7 jit_solution(12202687735140236729)
XLA Ops:
  0.6 1.4 %broadcast_in_dim.36 = bf16[16,4,8,128]{3,2,1,0:T(8,128)(2,1)} broadcast(bf16[4,8,128]{2,1,0:T(8,128)(2,1)} %bitcast.46), dimensions={1,2,3} | broadcast | bytes 139264 | tf_op jit(solution)/shard_map/broadcast_in_dim | solution.py:81
  2.0 9.0 %all-to-all-start = ((bf16[16,4,8,128]{3,2,1,0:T(8,128)(2,1)}), bf16[16,4,8,128]{3,2,1,0:T(8,128)(2,1)S(1)}, u32[]{:S(2)}, u32[]{:S(2)}) async-start(bf16[16,4,8,128]{3,2,1,0:T(8,128)(2,1)} %broadcast_in_dim.36), calls=%async_computation | async-start | bytes 262144 | tf_op jit(solution)/shard_map/all_to_all | solution.py:82
  11.7 0.8 compare_select_fusion.5.table_ref
  12.4 0.0 copy-start
  12.4 6.5 %all-to-all-done = bf16[16,4,8,128]{3,2,1,0:T(8,128)(2,1)S(1)} async-done(((bf16[16,4,8,128]{3,2,1,0:T(8,128)(2,1)}), bf16[16,4,8,128]{3,2,1,0:T(8,128)(2,1)S(1)}, u32[]{:S(2)}, u32[]{:S(2)}) %all-to-all-start) | async-done | bytes 131104 | tf_op jit(solution)/shard_map/all_to_all | solution.py:82
  18.9 0.0 copy-done
  18.9 0.0 copy-start.1
  18.9 1.7 %shard_map.87 = f32[128,8,128]{2,1,0:T(8,128)S(1)} custom-call(f32[128]{0:T(128)S(1)} %shard_map.86.table_ref, bf16[48,256,128]{2,1,0:T(8,128)(2,1)S(1)} %bitcast.33, bf16[64,8,128]{2,1,0:T(8,128)(2,1)S(1)} %bitcast.35), custom_call_target="tpu_custom_call" | custom-call | flops 25165824 | bytes 4194304 | tf_op jit(solution)/shard_map/pallas_call | solution.py:132
  20.6 4.2 %all-gather = f32[128,8,128]{2,1,0:T(8,128)S(1)} all-gather(f32[64,8,128]{2,1,0:T(8,128)S(1)} %slice.33), channel_id=2, replica_groups=mesh['zl'=4,'x'=4,'y'=4,'zh'=4,'c'=2] {'c'}, dimensions={0}, use_global_device_ids=true | all-gather | bytes 786432 | tf_op jit(solution)/shard_map/all_gather | solution.py:142
  24.9 9.3 %all_to_all.20 = f32[4,16,8,128]{3,2,1,0:T(8,128)S(1)} all-to-all(f32[4,16,8,128]{3,2,1,0:T(8,128)S(1)} %bitcast.38), channel_id=1, replica_groups=mesh['zl'=4,'x'=4,'y'=4,'zh'=4,'c'=2] {'y'}, dimensions={0} | all-to-all | bytes 524288 | tf_op jit(solution)/shard_map/all_to_all | solution.py:88
  34.2 0.0 copy-done.1
  34.2 14.1 %all-gather.1 = f32[34,8,128]{2,1,0:T(8,128)S(1)} all-gather(f32[17,8,128]{2,1,0:T(8,128)S(1)} %select_maximum_fusion), channel_id=3, replica_groups={{0,2},{4,6},{1,3},{5,7},{8,10},{12,14},{9,11},{13,15},{16,18},{20,22},{..., dimensions={0}, use_global_device_ids=true | all-gather | bytes 208896 | tf_op jit(solution)/shard_map/all_gather | solution.py:93
  48.3 7.8 %all-gather.2 = f32[34,8,128]{2,1,0:T(8,128)S(1)} all-gather(f32[17,8,128]{2,1,0:T(8,128)S(1)} %pad_maximum_fusion), channel_id=4, replica_groups={{0,6},{2,4},{1,7},{3,5},{8,14},{10,12},{9,15},{11,13},{16,22},{18,20},{..., dimensions={0}, use_global_device_ids=true | all-gather | bytes 208896 | tf_op jit(solution)/shard_map/all_gather | solution.py:93
  56.2 7.2 %all_to_all.21 = bf16[4,16,8,128]{3,2,1,0:T(8,128)(2,1)S(1)} all-to-all(bf16[4,16,8,128]{3,2,1,0:T(8,128)(2,1)S(1)} %broadcast_in_dim.38), channel_id=1, replica_groups=mesh['zl'=4,'x'=4,'y'=4,'zh'=4,'c'=2] {'y'}, dimensions={0} | all-to-all | bytes 262144 | tf_op jit(solution)/shard_map/all_to_all | solution.py:82
  63.4 4.3 %all_gather.27.scaled_ref = bf16[128,8,128]{2,1,0:T(8,128)(2,1)S(1)} all-gather(bf16[64,8,128]{2,1,0:T(8,128)(2,1)S(1)} %bitcast.43), channel_id=1, replica_groups=mesh['zl'=4,'x'=4,'y'=4,'zh'=4,'c'=2] {'c'}, dimensions={0}, use_global_device_ids=true | all-gather | bytes 393216 | tf_op jit(solution)/shard_map/all_gather | solution.py:151
  67.7 1.7 %shard_map.88 = (bf16[64,8,128]{2,1,0:T(8,128)(2,1)S(1)}, f32[4,8,128]{2,1,0:T(8,128)}) custom-call(f32[128]{0:T(128)S(1)} %shard_map.86.table_ref, bf16[48,256,128]{2,1,0:T(8,128)(2,1)S(1)} %bitcast.34, bf16[128,8,128]{2,1,0:T(8,128)(2,1)S(1)} %all_gather.27.scaled_ref, f32[16,8,128]{2,1,0:T(8,128)S(1)} %get-tuple-element.6.resid_ref), custom_call_target="tpu_custom_call" | custom-call | flops 25165824 | bytes 4194304 | tf_op jit(solution)/shard_map/pallas_call | solution.py:153
  69.5 13.6 %all_to_all.22 = bf16[16,4,8,128]{3,2,1,0:T(8,128)(2,1)S(1)} all-to-all(bf16[16,4,8,128]{3,2,1,0:T(8,128)(2,1)S(1)} %bitcast.36), channel_id=1, replica_groups=mesh['zl'=4,'x'=4,'y'=4,'zh'=4,'c'=2] {'zl','x'}, dimensions={0} | all-to-all | bytes 262144 | tf_op jit(solution)/shard_map/all_to_all | solution.py:88
  83.1 0.6 convert_reduce_fusion
  (11 shorter events, 0.1 us)
Async XLA Ops:
  2.0 16.9 %all-to-all-start = ((bf16[16,4,8,128]{3,2,1,0:T(8,128)(2,1)}), bf16[16,4,8,128]{3,2,1,0:T(8,128)(2,1)S(1)}, u32[]{:S(2)}, u32[]{:S(2)}) async-start(bf16[16,4,8,128]{3,2,1,0:T(8,128)(2,1)} %broadcast_in_dim.36), calls=%async_computation | async-start | bytes 262144 | tf_op jit(solution)/shard_map/all_to_all | solution.py:82
  12.4 6.5 %copy-start = (bf16[1,1,96,128,128]{4,3,2,1,0:T(8,128)(2,1)S(1)}, bf16[1,1,96,128,128]{4,3,2,1,0:T(8,128)(2,1)}, u32[]{:S(2)}) copy-start(bf16[1,1,96,128,128]{4,3,2,1,0:T(8,128)(2,1)} %param.10) | copy-start | bytes 9437188
  18.9 15.3 %copy-start.1 = (f32[512]{0:T(512)S(1)}, f32[512]{0:T(512)}, u32[]{:S(2)}) copy-start(f32[512]{0:T(512)} %param.8) | copy-start | bytes 6148

commit v6 on v5

--- a/solution.py
+++ b/solution.py
@@ -15,7 +15,7 @@
 
 def place(share, core):
     y, zh, c = share >> 3, (share >> 1) & 3, share & 1
-    return ((c ^ core) << 4) | (y << 2) | zh
+    return (y << 3) | ((c ^ core) << 2) | zh
 
 
 def settle(table_ref, out_ref):
@@ -62,7 +62,7 @@
     copy = pltpu.make_async_copy(own, own_ref, sem)
     copy.start()
     total[...] = jnp.zeros_like(total)
-    half = number(table_ref, AT_CORE) << 6
+    half = number(table_ref, AT_CORE) << 4
     for i in range(48):
         v, w = number(table_ref, 2 * i), number(table_ref, 2 * i + 1)
         a, b = scaled_ref[((v >> 8) & 127) ^ half], scaled_ref[((w >> 8) & 127) ^ half]
@@ -139,16 +139,17 @@
         cost_estimate=cost,
     )(table, tiles_here, x_all)
 
-    halves = lax.all_gather(partial[64:], "c")
-    partial = partial[:64] + lax.dynamic_index_in_dim(halves, 1 - core, 0, keepdims=False)
-    partial = sum_shares(partial, "y")
-    got = gather_pairs(partial, diag_rows.reshape(1, 4, width), [[0, 1], [2, 3]])
+    partial = partial.reshape(4, 2, 16, 8, width)
+    halves = lax.all_gather(partial[:, 1], "c")
+    partial = partial[:, 0] + lax.dynamic_index_in_dim(halves, 1 - core, 0, keepdims=False)
+    partial = jnp.sum(lax.all_to_all(partial, "y", 0, 0), axis=0)
+    got = gather_pairs(partial, diag_rows.reshape(1, 4, width), [[0, 3], [1, 2]])
     diag = got[:, 16, :4].reshape(1, 8, width)
-    got = gather_pairs(got[0, :16] + got[1, :16], diag, [[0, 3], [1, 2]])
+    got = gather_pairs(got[0, :16] + got[1, :16], diag, [[0, 1], [3, 2]])
     resid = got[0, :16] + got[1, :16]
-    diag = got[:, 16].reshape(16, 1, width)
-    scaled = to_all((resid / diag).astype(jnp.bfloat16), "y").reshape(64, 8, width)
-    scaled = lax.all_gather(scaled, "c", tiled=True)
+    diag = got[:, 16]
+    diag = jnp.concatenate([diag[0, :4], diag[1], diag[0, 4:]], axis=0).reshape(16, 1, width)
+    scaled = to_all((resid / diag).astype(jnp.bfloat16), ("y", "c")).reshape(128, 8, width)
 
     back, resid = pl.pallas_call(
         backward,

time: 84.1 us -> 82.2 us (0.977)
  blocking collectives: 60.5 us -> 58.6 us
    all_to_all x2 -> x1, blocking collectives: 22.9 us -> 10.6 us  [sum_shares(): lax.all_to_all(parts, axes, 0, 0).astype(jnp.float32)]
    all_to_all x0 -> x1, blocking collectives: none -> 9.27 us  [body(): partial = jnp.sum(lax.all_to_all(partial, 'y', 0, 0), axis=0)]
    all_gather x2 -> x1, blocking collectives: 8.49 us -> 4.18 us  [body(): halves = lax.all_gather(partial[:, 1], 'c')]
    all_gather x2, blocking collectives: 21.9 us -> 24.9 us  [gather_pairs(): lax.all_gather(jnp.concatenate([partial, diag], axis=0), 'zh', axis_index...]
    all_to_all x1, blocking collectives: 7.21 us -> 9.54 us  [to_all(): return lax.all_to_all(copies, axes, 0, 0)]
where the time goes in v6:
time: 82.2 us; the launch traced here: 81.8 us
  blocking collectives  58.6 us (71%)
  starting transfers between devices  9.01 us (11%)
  waiting for transfers between devices  6.47 us (8%)
  Pallas kernels  3.48 us (4%)
  other arithmetic  1.5 us (2%)
  local copies, waits for them, and re-layouts  1.42 us (2%)
  between operations  1.38 us (2%)
    all_gather x2, blocking collectives, gather_pairs(): lax.all_gather(jnp.concatenate([partial, diag], axis=0), 'zh', axis_index...  24.9 us
    all_to_all x1, blocking collectives, sum_shares(): lax.all_to_all(parts, axes, 0, 0).astype(jnp.float32)  10.6 us
    all_to_all x1, blocking collectives, to_all(): return lax.all_to_all(copies, axes, 0, 0)  9.54 us
    all_to_all x1, blocking collectives, body(): partial = jnp.sum(lax.all_to_all(partial, 'y', 0, 0), axis=0)  9.27 us
    all_to_all x1, starting transfers between devices, to_all(): return lax.all_to_all(copies, axes, 0, 0)  9.01 us
    all_to_all x1, waiting for transfers between devices, to_all(): return lax.all_to_all(copies, axes, 0, 0)  6.47 us
    all_gather x1, blocking collectives, body(): halves = lax.all_gather(partial[:, 1], 'c')  4.18 us
    pallas_call x1, Pallas kernels, body(): pl.pallas_call(backward, out_shape=(jax.ShapeDtypeStruct((64, 8, width),...  1.77 us
  transfers between devices with their start and end apart: 1, of which 1 were waited for; matrix products, arithmetic and copies ran while one was open for 1% of the time, Pallas kernels for 0%

profile of v6, /device:TPU:1, one launch (start us, length us, event | category | flops | bytes accessed | tf_op | source)
XLA Modules:
  0.0 81.8 jit_solution(6747992245425927045)
XLA Ops:
  0.6 1.3 %broadcast_in_dim.36 = bf16[16,4,8,128]{3,2,1,0:T(8,128)(2,1)} broadcast(bf16[4,8,128]{2,1,0:T(8,128)(2,1)} %bitcast.60), dimensions={1,2,3} | broadcast | bytes 139264 | tf_op jit(solution)/shard_map/broadcast_in_dim | solution.py:81
  2.0 9.0 %all-to-all-start = ((bf16[16,4,8,128]{3,2,1,0:T(8,128)(2,1)}), bf16[16,4,8,128]{3,2,1,0:T(8,128)(2,1)S(1)}, u32[]{:S(2)}, u32[]{:S(2)}) async-start(bf16[16,4,8,128]{3,2,1,0:T(8,128)(2,1)} %broadcast_in_dim.36), calls=%async_computation | async-start | bytes 262144 | tf_op jit(solution)/shard_map/all_to_all | solution.py:82
  11.7 0.8 compare_select_fusion.5.table_ref
  12.4 0.0 copy-start
  12.4 6.5 %all-to-all-done = bf16[16,4,8,128]{3,2,1,0:T(8,128)(2,1)S(1)} async-done(((bf16[16,4,8,128]{3,2,1,0:T(8,128)(2,1)}), bf16[16,4,8,128]{3,2,1,0:T(8,128)(2,1)S(1)}, u32[]{:S(2)}, u32[]{:S(2)}) %all-to-all-start) | async-done | bytes 131104 | tf_op jit(solution)/shard_map/all_to_all | solution.py:82
  18.9 0.0 copy-done
  18.9 0.0 copy-start.1
  18.9 1.7 %shard_map.87 = f32[128,8,128]{2,1,0:T(8,128)S(1)} custom-call(f32[128]{0:T(128)S(1)} %shard_map.86.table_ref, bf16[48,256,128]{2,1,0:T(8,128)(2,1)S(1)} %bitcast.45, bf16[64,8,128]{2,1,0:T(8,128)(2,1)S(1)} %bitcast.50), custom_call_target="tpu_custom_call" | custom-call | flops 25165824 | bytes 4194304 | tf_op jit(solution)/shard_map/pallas_call | solution.py:132
  20.7 4.2 %all-gather = f32[8,1,16,8,128]{4,3,2,1,0:T(8,128)S(1)} all-gather(f32[4,1,16,8,128]{4,3,2,1,0:T(8,128)S(1)} %slice.47), channel_id=2, replica_groups=mesh['zl'=4,'x'=4,'y'=4,'zh'=4,'c'=2] {'c'}, dimensions={0}, use_global_device_ids=true | all-gather | bytes 786432 | tf_op jit(solution)/shard_map/all_gather | solution.py:143
  24.9 9.3 %all_to_all.20 = f32[4,16,8,128]{3,2,1,0:T(8,128)S(1)} all-to-all(f32[4,16,8,128]{3,2,1,0:T(8,128)S(1)} %fusion), channel_id=1, replica_groups=mesh['zl'=4,'x'=4,'y'=4,'zh'=4,'c'=2] {'y'}, dimensions={0} | all-to-all | bytes 524288 | tf_op jit(solution)/shard_map/all_to_all | solution.py:145
  34.2 0.0 copy-done.1
  34.2 14.1 %all-gather.1 = f32[34,8,128]{2,1,0:T(8,128)S(1)} all-gather(f32[17,8,128]{2,1,0:T(8,128)S(1)} %select_maximum_fusion), channel_id=3, replica_groups={{0,6},{2,4},{1,7},{3,5},{8,14},{10,12},{9,15},{11,13},{16,22},{18,20},{..., dimensions={0}, use_global_device_ids=true | all-gather | bytes 208896 | tf_op jit(solution)/shard_map/all_gather | solution.py:93
  48.3 10.8 %all-gather.2 = f32[34,8,128]{2,1,0:T(8,128)S(1)} all-gather(f32[17,8,128]{2,1,0:T(8,128)S(1)} %pad_maximum_fusion), channel_id=4, replica_groups={{0,2},{6,4},{1,3},{7,5},{8,10},{14,12},{9,11},{15,13},{16,18},{22,20},{..., dimensions={0}, use_global_device_ids=true | all-gather | bytes 208896 | tf_op jit(solution)/shard_map/all_gather | solution.py:93
  59.3 9.5 %all_to_all.21 = bf16[8,16,8,128]{3,2,1,0:T(8,128)(2,1)S(1)} all-to-all(bf16[8,16,8,128]{3,2,1,0:T(8,128)(2,1)S(1)} %broadcast_in_dim.38), channel_id=1, replica_groups=mesh['zl'=4,'x'=4,'y'=4,'zh'=4,'c'=2] {'y','c'}, dimensions={0} | all-to-all | bytes 524288 | tf_op jit(solution)/shard_map/all_to_all | solution.py:82
  68.8 1.8 %shard_map.88 = (bf16[64,8,128]{2,1,0:T(8,128)(2,1)S(1)}, f32[4,8,128]{2,1,0:T(8,128)}) custom-call(f32[128]{0:T(128)S(1)} %shard_map.86.table_ref, bf16[48,256,128]{2,1,0:T(8,128)(2,1)S(1)} %bitcast.46, bf16[128,8,128]{2,1,0:T(8,128)(2,1)S(1)} %bitcast.49, f32[16,8,128]{2,1,0:T(8,128)S(1)} %get-tuple-element.6.resid_ref), custom_call_target="tpu_custom_call" | custom-call | flops 25165824 | bytes 4194304 | tf_op jit(solution)/shard_map/pallas_call | solution.py:154
  70.6 10.6 %all_to_all.22 = bf16[16,4,8,128]{3,2,1,0:T(8,128)(2,1)S(1)} all-to-all(bf16[16,4,8,128]{3,2,1,0:T(8,128)(2,1)S(1)} %bitcast.51), channel_id=1, replica_groups=mesh['zl'=4,'x'=4,'y'=4,'zh'=4,'c'=2] {'zl','x'}, dimensions={0} | all-to-all | bytes 262144 | tf_op jit(solution)/shard_map/all_to_all | solution.py:88
  81.2 0.6 convert_reduce_fusion
  (14 shorter events, 0.2 us)
Async XLA Ops:
  2.0 16.9 %all-to-all-start = ((bf16[16,4,8,128]{3,2,1,0:T(8,128)(2,1)}), bf16[16,4,8,128]{3,2,1,0:T(8,128)(2,1)S(1)}, u32[]{:S(2)}, u32[]{:S(2)}) async-start(bf16[16,4,8,128]{3,2,1,0:T(8,128)(2,1)} %broadcast_in_dim.36), calls=%async_computation | async-start | bytes 262144 | tf_op jit(solution)/shard_map/all_to_all | solution.py:82
  12.4 6.5 %copy-start = (bf16[1,1,96,128,128]{4,3,2,1,0:T(8,128)(2,1)S(1)}, bf16[1,1,96,128,128]{4,3,2,1,0:T(8,128)(2,1)}, u32[]{:S(2)}) copy-start(bf16[1,1,96,128,128]{4,3,2,1,0:T(8,128)(2,1)} %param.10) | copy-start | bytes 9437188
  18.9 15.3 %copy-start.1 = (f32[512]{0:T(512)S(1)}, f32[512]{0:T(512)}, u32[]{:S(2)}) copy-start(f32[512]{0:T(512)} %param.8) | copy-start | bytes 6148

commit v7 on v6

--- a/solution.py
+++ b/solution.py
@@ -57,10 +57,8 @@
     out_ref[...] = total[:128]
 
 
-def backward(table_ref, tiles_ref, scaled_ref, resid_ref, out_ref, own_ref, total, sem):
-    own = resid_ref.at[pl.ds(number(table_ref, AT_ZH) * 4, 4)]
-    copy = pltpu.make_async_copy(own, own_ref, sem)
-    copy.start()
+def backward(table_ref, tiles_ref, scaled_ref, resid_ref, out_ref, own_ref, total):
+    own_ref[...] = resid_ref[pl.ds(number(table_ref, AT_ZH) * 4, 4)]
     total[...] = jnp.zeros_like(total)
     half = number(table_ref, AT_CORE) << 4
     for i in range(48):
@@ -74,18 +72,16 @@
         total[v & 255] = total[v & 255] + part[:8]
         total[w & 255] = total[w & 255] + part[8:]
     out_ref[...] = total[:64].astype(out_ref.dtype)
-    copy.wait()
+
+
+def finish(parts_ref, own_ref, image_ref, resid_ref):
+    resid_ref[...] = own_ref[...]
+    image_ref[...] = jnp.sum(parts_ref[...].astype(jnp.float32), axis=0)
 
 
 def to_all(own, axes):
     copies = jnp.broadcast_to(own[None], (lax.axis_size(axes), *own.shape))
     return lax.all_to_all(copies, axes, 0, 0)
-
-
-def sum_shares(parts, axes):
-    n = lax.axis_size(axes)
-    parts = parts.reshape(n, parts.shape[0] // n, *parts.shape[1:])
-    return jnp.sum(lax.all_to_all(parts, axes, 0, 0).astype(jnp.float32), axis=0)
 
 
 def gather_pairs(partial, diag, pairs):
@@ -153,14 +149,21 @@
 
     back, resid = pl.pallas_call(
         backward,
-        out_shape=(jax.ShapeDtypeStruct((64, 8, width), BACK), f32((4, 8, width))),
+        out_shape=(jax.ShapeDtypeStruct((64, 8, width), BACK), pltpu.VMEM((4, 8, width), jnp.float32)),
         in_specs=[smem, vmem, vmem, vmem],
-        out_specs=(vmem, pl.BlockSpec(memory_space=pl.ANY)),
-        scratch_shapes=[pltpu.VMEM((72, 8, width), jnp.float32), pltpu.SemaphoreType.DMA],
+        out_specs=(vmem, vmem),
+        scratch_shapes=[pltpu.VMEM((72, 8, width), jnp.float32)],
         compiler_params=params,
         cost_estimate=cost,
     )(table, tiles_here, scaled, resid)
-    return vectors_of(resid), vectors_of(sum_shares(back, ROW))
+    image, resid = pl.pallas_call(
+        finish,
+        out_shape=(f32((4, 8, width)), f32((4, 8, width))),
+        in_specs=[vmem, vmem],
+        out_specs=(vmem, vmem),
+        compiler_params=params,
+    )(lax.all_to_all(back.reshape(16, 4, 8, width), ROW, 0, 0), resid)
+    return vectors_of(resid), vectors_of(image)
 
 
 def solution(mesh):

time: 82.2 us -> 81.8 us (level)
  no operation moved by 1% of the time
where the time goes in v7:
time: 81.8 us; the launch traced here: 81.4 us
  blocking collectives  58.7 us (72%)
  starting transfers between devices  9.01 us (11%)
  waiting for transfers between devices  6.47 us (8%)
  Pallas kernels  3.54 us (4%)
  local copies, waits for them, and re-layouts  1.43 us (2%)
  between operations  1.38 us (2%)
  other arithmetic  0.88 us (1%)
    all_gather x2, blocking collectives, gather_pairs(): lax.all_gather(jnp.concatenate([partial, diag], axis=0), 'zh', axis_index...  25.1 us
    all_to_all x1, blocking collectives, body(): lax.all_to_all(back.reshape(16, 4, 8, width), ROW, 0, 0)  10.7 us
    all_to_all x1, blocking collectives, to_all(): return lax.all_to_all(copies, axes, 0, 0)  9.4 us
    all_to_all x1, blocking collectives, body(): partial = jnp.sum(lax.all_to_all(partial, 'y', 0, 0), axis=0)  9.26 us
    all_to_all x1, starting transfers between devices, to_all(): return lax.all_to_all(copies, axes, 0, 0)  9.01 us
    all_to_all x1, waiting for transfers between devices, to_all(): return lax.all_to_all(copies, axes, 0, 0)  6.47 us
    all_gather x1, blocking collectives, body(): halves = lax.all_gather(partial[:, 1], 'c')  4.18 us
    pallas_call x1, Pallas kernels, body(): pl.pallas_call(forward, out_shape=f32((128, 8, width)), in_specs=[smem, v...  1.69 us
  transfers between devices with their start and end apart: 1, of which 1 were waited for; matrix products, arithmetic and copies ran while one was open for 1% of the time, Pallas kernels for 0%

profile of v7, /device:TPU:1, one launch (start us, length us, event | category | flops | bytes accessed | tf_op | source)
XLA Modules:
  0.0 81.4 jit_solution(5478547008724675861)
XLA Ops:
  0.6 1.4 %broadcast_in_dim.36 = bf16[16,4,8,128]{3,2,1,0:T(8,128)(2,1)} broadcast(bf16[4,8,128]{2,1,0:T(8,128)(2,1)} %bitcast.59), dimensions={1,2,3} | broadcast | bytes 139264 | tf_op jit(solution)/shard_map/broadcast_in_dim | solution.py:83
  2.0 9.0 %all-to-all-start = ((bf16[16,4,8,128]{3,2,1,0:T(8,128)(2,1)}), bf16[16,4,8,128]{3,2,1,0:T(8,128)(2,1)S(1)}, u32[]{:S(2)}, u32[]{:S(2)}) async-start(bf16[16,4,8,128]{3,2,1,0:T(8,128)(2,1)} %broadcast_in_dim.36), calls=%async_computation | async-start | bytes 262144 | tf_op jit(solution)/shard_map/all_to_all | solution.py:84
  11.7 0.8 compare_select_fusion.5.table_ref
  12.4 0.0 copy-start
  12.4 6.5 %all-to-all-done = bf16[16,4,8,128]{3,2,1,0:T(8,128)(2,1)S(1)} async-done(((bf16[16,4,8,128]{3,2,1,0:T(8,128)(2,1)}), bf16[16,4,8,128]{3,2,1,0:T(8,128)(2,1)S(1)}, u32[]{:S(2)}, u32[]{:S(2)}) %all-to-all-start) | async-done | bytes 131104 | tf_op jit(solution)/shard_map/all_to_all | solution.py:84
  18.9 0.0 copy-done
  18.9 0.0 copy-start.1
  18.9 1.7 %shard_map.87 = f32[128,8,128]{2,1,0:T(8,128)S(1)} custom-call(f32[128]{0:T(128)S(1)} %shard_map.86.table_ref, bf16[48,256,128]{2,1,0:T(8,128)(2,1)S(1)} %bitcast.45, bf16[64,8,128]{2,1,0:T(8,128)(2,1)S(1)} %bitcast.50), custom_call_target="tpu_custom_call" | custom-call | flops 25165824 | bytes 4194304 | tf_op jit(solution)/shard_map/pallas_call | solution.py:128
  20.6 4.2 %all-gather = f32[8,1,16,8,128]{4,3,2,1,0:T(8,128)S(1)} all-gather(f32[4,1,16,8,128]{4,3,2,1,0:T(8,128)S(1)} %slice.47), channel_id=2, replica_groups=mesh['zl'=4,'x'=4,'y'=4,'zh'=4,'c'=2] {'c'}, dimensions={0}, use_global_device_ids=true | all-gather | bytes 786432 | tf_op jit(solution)/shard_map/all_gather | solution.py:139
  24.9 9.3 %all_to_all.20 = f32[4,16,8,128]{3,2,1,0:T(8,128)S(1)} all-to-all(f32[4,16,8,128]{3,2,1,0:T(8,128)S(1)} %fusion), channel_id=1, replica_groups=mesh['zl'=4,'x'=4,'y'=4,'zh'=4,'c'=2] {'y'}, dimensions={0} | all-to-all | bytes 524288 | tf_op jit(solution)/shard_map/all_to_all | solution.py:141
  34.1 0.0 copy-done.1
  34.2 14.2 %all-gather.1 = f32[34,8,128]{2,1,0:T(8,128)S(1)} all-gather(f32[17,8,128]{2,1,0:T(8,128)S(1)} %select_maximum_fusion), channel_id=3, replica_groups={{0,6},{2,4},{1,7},{3,5},{8,14},{10,12},{9,15},{11,13},{16,22},{18,20},{..., dimensions={0}, use_global_device_ids=true | all-gather | bytes 208896 | tf_op jit(solution)/shard_map/all_gather | solution.py:89
  48.4 11.0 %all-gather.2 = f32[34,8,128]{2,1,0:T(8,128)S(1)} all-gather(f32[17,8,128]{2,1,0:T(8,128)S(1)} %pad_maximum_fusion), channel_id=4, replica_groups={{0,2},{6,4},{1,3},{7,5},{8,10},{14,12},{9,11},{15,13},{16,18},{22,20},{..., dimensions={0}, use_global_device_ids=true | all-gather | bytes 208896 | tf_op jit(solution)/shard_map/all_gather | solution.py:89
  59.4 9.4 %all_to_all.21 = bf16[8,16,8,128]{3,2,1,0:T(8,128)(2,1)S(1)} all-to-all(bf16[8,16,8,128]{3,2,1,0:T(8,128)(2,1)S(1)} %broadcast_in_dim.38), channel_id=1, replica_groups=mesh['zl'=4,'x'=4,'y'=4,'zh'=4,'c'=2] {'y','c'}, dimensions={0} | all-to-all | bytes 524288 | tf_op jit(solution)/shard_map/all_to_all | solution.py:84
  68.8 1.2 %shard_map.88 = (bf16[64,8,128]{2,1,0:T(8,128)(2,1)S(1)}, f32[4,8,128]{2,1,0:T(8,128)S(1)}) custom-call(f32[128]{0:T(128)S(1)} %shard_map.86.table_ref, bf16[48,256,128]{2,1,0:T(8,128)(2,1)S(1)} %bitcast.46, bf16[128,8,128]{2,1,0:T(8,128)(2,1)S(1)} %bitcast.49, f32[16,8,128]{2,1,0:T(8,128)S(1)} %get-tuple-element.10.resid_ref), custom_call_target="tpu_custom_call" | custom-call | flops 25165824 | bytes 4194304 | tf_op jit(solution)/shard_map/pallas_call | solution.py:150
  70.0 10.7 %all_to_all.22.parts_ref = bf16[16,4,8,128]{3,2,1,0:T(8,128)(2,1)S(1)} all-to-all(bf16[16,4,8,128]{3,2,1,0:T(8,128)(2,1)S(1)} %bitcast.51), channel_id=1, replica_groups=mesh['zl'=4,'x'=4,'y'=4,'zh'=4,'c'=2] {'zl','x'}, dimensions={0} | all-to-all | bytes 262144 | tf_op jit(solution)/shard_map/all_to_all | solution.py:165
  80.8 0.6 shard_map.89
  (14 shorter events, 0.2 us)
Async XLA Ops:
  2.0 16.9 %all-to-all-start = ((bf16[16,4,8,128]{3,2,1,0:T(8,128)(2,1)}), bf16[16,4,8,128]{3,2,1,0:T(8,128)(2,1)S(1)}, u32[]{:S(2)}, u32[]{:S(2)}) async-start(bf16[16,4,8,128]{3,2,1,0:T(8,128)(2,1)} %broadcast_in_dim.36), calls=%async_computation | async-start | bytes 262144 | tf_op jit(solution)/shard_map/all_to_all | solution.py:84
  12.4 6.5 %copy-start = (bf16[1,1,96,128,128]{4,3,2,1,0:T(8,128)(2,1)S(1)}, bf16[1,1,96,128,128]{4,3,2,1,0:T(8,128)(2,1)}, u32[]{:S(2)}) copy-start(bf16[1,1,96,128,128]{4,3,2,1,0:T(8,128)(2,1)} %param.10) | copy-start | bytes 9437188
  18.9 15.2 %copy-start.1 = (f32[512]{0:T(512)S(1)}, f32[512]{0:T(512)}, u32[]{:S(2)}) copy-start(f32[512]{0:T(512)} %param.8) | copy-start | bytes 6148

commit v8 on v7

--- a/solution.py
+++ b/solution.py
@@ -26,7 +26,7 @@
     return table_ref[at].astype(jnp.int32)
 
 
-def forward(table_ref, tiles_ref, x_ref, out_ref, total):
+def forward(table_ref, tiles_ref, x_ref, own_ref, other_ref, total):
     total[...] = jnp.zeros_like(total)
     row, col = number(table_ref, AT_ROW), number(table_ref, AT_COL)
 
@@ -38,23 +38,26 @@
         for n in range(8):
             theta = jnp.where(line == n, table_ref[AT_THETA + n], theta)
 
-        def shift(s, carry):
+        for s in range(16):
             p = place(first + s, col & 1) * 4
             for j in range(4):
                 total[p + j] = -theta * x_ref[s * 4 + j].astype(jnp.float32)
-            return carry
 
-        lax.fori_loop(0, 16, shift, 0)
-
+    parts = []
     for i in range(48):
         v, w = number(table_ref, 2 * i), number(table_ref, 2 * i + 1)
         both = jnp.concatenate([x_ref[v & 63], x_ref[w & 63]], axis=0)
         part = lax.dot_general(
             both, tiles_ref[i], (((1,), (1,)), ((), ())), preferred_element_type=jnp.float32
         )
-        total[v >> 8] = total[v >> 8] + part[:8, :128]
-        total[w >> 8] = total[w >> 8] + part[8:, 128:]
-    out_ref[...] = total[:128]
+        parts += [(v >> 8, part[:8, :128]), (w >> 8, part[8:, 128:])]
+        if len(parts) == 16:
+            for p, part in parts:
+                total[p] = total[p] + part
+            parts = []
+    for y in range(4):
+        own_ref[y] = total[y * 32 : y * 32 + 16]
+        other_ref[y] = total[y * 32 + 16 : y * 32 + 32]
 
 
 def backward(table_ref, tiles_ref, scaled_ref, resid_ref, out_ref, own_ref, total):
@@ -125,19 +128,18 @@
 
     own = x_cols.reshape(8, 4, width).transpose(1, 0, 2)
     x_all = to_all(own, ROW).reshape(64, 8, width)
-    partial = pl.pallas_call(
+    partial, other = pl.pallas_call(
         forward,
-        out_shape=f32((128, 8, width)),
+        out_shape=(f32((4, 16, 8, width)), f32((4, 16, 8, width))),
         in_specs=[smem, vmem, vmem],
-        out_specs=vmem,
+        out_specs=(vmem, vmem),
         scratch_shapes=[pltpu.VMEM((136, 8, width), jnp.float32)],
         compiler_params=params,
         cost_estimate=cost,
     )(table, tiles_here, x_all)
 
-    partial = partial.reshape(4, 2, 16, 8, width)
-    halves = lax.all_gather(partial[:, 1], "c")
-    partial = partial[:, 0] + lax.dynamic_index_in_dim(halves, 1 - core, 0, keepdims=False)
+    halves = lax.all_gather(other, "c")
+    partial = partial + lax.dynamic_index_in_dim(halves, 1 - core, 0, keepdims=False)
     partial = jnp.sum(lax.all_to_all(partial, "y", 0, 0), axis=0)
     got = gather_pairs(partial, diag_rows.reshape(1, 4, width), [[0, 3], [1, 2]])
     diag = got[:, 16, :4].reshape(1, 8, width)

time: 81.8 us -> 81.7 us (level)
  no operation moved by 1% of the time
where the time goes in v8:
time: 81.7 us; the launch traced here: 81.3 us
  blocking collectives  58.7 us (72%)
  starting transfers between devices  9.01 us (11%)
  waiting for transfers between devices  6.47 us (8%)
  Pallas kernels  3.48 us (4%)
  local copies, waits for them, and re-layouts  1.42 us (2%)
  between operations  1.37 us (2%)
  other arithmetic  0.87 us (1%)
    all_gather x2, blocking collectives, gather_pairs(): lax.all_gather(jnp.concatenate([partial, diag], axis=0), 'zh', axis_index...  24.9 us
    all_to_all x1, blocking collectives, body(): lax.all_to_all(back.reshape(16, 4, 8, width), ROW, 0, 0)  10.7 us
    all_to_all x1, blocking collectives, to_all(): return lax.all_to_all(copies, axes, 0, 0)  9.55 us
    all_to_all x1, blocking collectives, body(): partial = jnp.sum(lax.all_to_all(partial, 'y', 0, 0), axis=0)  9.33 us
    all_to_all x1, starting transfers between devices, to_all(): return lax.all_to_all(copies, axes, 0, 0)  9.01 us
    all_to_all x1, waiting for transfers between devices, to_all(): return lax.all_to_all(copies, axes, 0, 0)  6.47 us
    all_gather x1, blocking collectives, body(): halves = lax.all_gather(other, 'c')  4.19 us
  transfers between devices with their start and end apart: 1, of which 1 were waited for; matrix products, arithmetic and copies ran while one was open for 1% of the time, Pallas kernels for 0%

profile of v8, /device:TPU:1, one launch (start us, length us, event | category | flops | bytes accessed | tf_op | source)
XLA Modules:
  0.0 81.3 jit_solution(10593271385938473096)
XLA Ops:
  0.6 1.4 %broadcast_in_dim.36 = bf16[16,4,8,128]{3,2,1,0:T(8,128)(2,1)} broadcast(bf16[4,8,128]{2,1,0:T(8,128)(2,1)} %bitcast.52), dimensions={1,2,3} | broadcast | bytes 139264 | tf_op jit(solution)/shard_map/broadcast_in_dim | solution.py:86
  2.0 9.0 %all-to-all-start = ((bf16[16,4,8,128]{3,2,1,0:T(8,128)(2,1)}), bf16[16,4,8,128]{3,2,1,0:T(8,128)(2,1)S(1)}, u32[]{:S(2)}, u32[]{:S(2)}) async-start(bf16[16,4,8,128]{3,2,1,0:T(8,128)(2,1)} %broadcast_in_dim.36), calls=%async_computation | async-start | bytes 262144 | tf_op jit(solution)/shard_map/all_to_all | solution.py:87
  11.7 0.8 compare_select_fusion.5.table_ref
  12.4 0.0 copy-start
  12.4 0.0 copy-start.1
  12.4 6.5 %all-to-all-done = bf16[16,4,8,128]{3,2,1,0:T(8,128)(2,1)S(1)} async-done(((bf16[16,4,8,128]{3,2,1,0:T(8,128)(2,1)}), bf16[16,4,8,128]{3,2,1,0:T(8,128)(2,1)S(1)}, u32[]{:S(2)}, u32[]{:S(2)}) %all-to-all-start) | async-done | bytes 131104 | tf_op jit(solution)/shard_map/all_to_all | solution.py:87
  18.9 0.0 copy-done
  18.9 1.6 %shard_map.87 = (f32[4,16,8,128]{3,2,1,0:T(8,128)S(1)}, f32[4,16,8,128]{3,2,1,0:T(8,128)S(1)}) custom-call(f32[128]{0:T(128)S(1)} %shard_map.86.table_ref, bf16[48,256,128]{2,1,0:T(8,128)(2,1)S(1)} %bitcast.40, bf16[64,8,128]{2,1,0:T(8,128)(2,1)S(1)} %bitcast.43), custom_call_target="tpu_custom_call" | custom-call | flops 25165824 | bytes 4194304 | tf_op jit(solution)/shard_map/pallas_call | solution.py:131
  20.6 4.2 %all-gather = f32[8,16,8,128]{3,2,1,0:T(8,128)S(1)} all-gather(f32[4,16,8,128]{3,2,1,0:T(8,128)S(1)} %get-tuple-element.9), channel_id=2, replica_groups=mesh['zl'=4,'x'=4,'y'=4,'zh'=4,'c'=2] {'c'}, dimensions={0}, use_global_device_ids=true | all-gather | bytes 786432 | tf_op jit(solution)/shard_map/all_gather | solution.py:141
  24.8 9.3 %all_to_all.20 = f32[4,16,8,128]{3,2,1,0:T(8,128)S(1)} all-to-all(f32[4,16,8,128]{3,2,1,0:T(8,128)S(1)} %bitcast_add_fusion), channel_id=1, replica_groups=mesh['zl'=4,'x'=4,'y'=4,'zh'=4,'c'=2] {'y'}, dimensions={0} | all-to-all | bytes 524288 | tf_op jit(solution)/shard_map/all_to_all | solution.py:143
  34.1 0.0 copy-done.1
  34.2 14.1 %all-gather.1 = f32[34,8,128]{2,1,0:T(8,128)S(1)} all-gather(f32[17,8,128]{2,1,0:T(8,128)S(1)} %select_maximum_fusion), channel_id=3, replica_groups={{0,6},{2,4},{1,7},{3,5},{8,14},{10,12},{9,15},{11,13},{16,22},{18,20},{..., dimensions={0}, use_global_device_ids=true | all-gather | bytes 208896 | tf_op jit(solution)/shard_map/all_gather | solution.py:92
  48.3 10.8 %all-gather.2 = f32[34,8,128]{2,1,0:T(8,128)S(1)} all-gather(f32[17,8,128]{2,1,0:T(8,128)S(1)} %pad_maximum_fusion), channel_id=4, replica_groups={{0,2},{6,4},{1,3},{7,5},{8,10},{14,12},{9,11},{15,13},{16,18},{22,20},{..., dimensions={0}, use_global_device_ids=true | all-gather | bytes 208896 | tf_op jit(solution)/shard_map/all_gather | solution.py:92
  59.2 9.5 %all_to_all.21 = bf16[8,16,8,128]{3,2,1,0:T(8,128)(2,1)S(1)} all-to-all(bf16[8,16,8,128]{3,2,1,0:T(8,128)(2,1)S(1)} %broadcast_in_dim.38), channel_id=1, replica_groups=mesh['zl'=4,'x'=4,'y'=4,'zh'=4,'c'=2] {'y','c'}, dimensions={0} | all-to-all | bytes 524288 | tf_op jit(solution)/shard_map/all_to_all | solution.py:87
  68.8 1.2 %shard_map.88 = (bf16[64,8,128]{2,1,0:T(8,128)(2,1)S(1)}, f32[4,8,128]{2,1,0:T(8,128)S(1)}) custom-call(f32[128]{0:T(128)S(1)} %shard_map.86.table_ref, bf16[48,256,128]{2,1,0:T(8,128)(2,1)S(1)} %bitcast.41, bf16[128,8,128]{2,1,0:T(8,128)(2,1)S(1)} %bitcast.42, f32[16,8,128]{2,1,0:T(8,128)S(1)} %get-tuple-element.14.resid_ref), custom_call_target="tpu_custom_call" | custom-call | flops 25165824 | bytes 4194304 | tf_op jit(solution)/shard_map/pallas_call | solution.py:152
  70.0 10.7 %all_to_all.22.parts_ref = bf16[16,4,8,128]{3,2,1,0:T(8,128)(2,1)S(1)} all-to-all(bf16[16,4,8,128]{3,2,1,0:T(8,128)(2,1)S(1)} %bitcast.44), channel_id=1, replica_groups=mesh['zl'=4,'x'=4,'y'=4,'zh'=4,'c'=2] {'zl','x'}, dimensions={0} | all-to-all | bytes 262144 | tf_op jit(solution)/shard_map/all_to_all | solution.py:167
  80.7 0.6 shard_map.89
  (13 shorter events, 0.2 us)
Async XLA Ops:
  2.0 16.9 %all-to-all-start = ((bf16[16,4,8,128]{3,2,1,0:T(8,128)(2,1)}), bf16[16,4,8,128]{3,2,1,0:T(8,128)(2,1)S(1)}, u32[]{:S(2)}, u32[]{:S(2)}) async-start(bf16[16,4,8,128]{3,2,1,0:T(8,128)(2,1)} %broadcast_in_dim.36), calls=%async_computation | async-start | bytes 262144 | tf_op jit(solution)/shard_map/all_to_all | solution.py:87
  12.4 6.5 %copy-start = (bf16[1,1,96,128,128]{4,3,2,1,0:T(8,128)(2,1)S(1)}, bf16[1,1,96,128,128]{4,3,2,1,0:T(8,128)(2,1)}, u32[]{:S(2)}) copy-start(bf16[1,1,96,128,128]{4,3,2,1,0:T(8,128)(2,1)} %param.10) | copy-start | bytes 9437188
  12.4 21.7 %copy-start.1 = (f32[512]{0:T(512)S(1)}, f32[512]{0:T(512)}, u32[]{:S(2)}) copy-start(f32[512]{0:T(512)} %param.8) | copy-start | bytes 6148

commit v9 on v7

--- a/solution.py
+++ b/solution.py
@@ -26,8 +26,11 @@
     return table_ref[at].astype(jnp.int32)
 
 
-def forward(table_ref, tiles_ref, x_ref, out_ref, total):
+def forward(table_in, tiles_ref, x_ref, out_ref, total, table_ref, sem):
+    copy = pltpu.make_async_copy(table_in, table_ref, sem)
+    copy.start()
     total[...] = jnp.zeros_like(total)
+    copy.wait()
     row, col = number(table_ref, AT_ROW), number(table_ref, AT_COL)
 
     @pl.when(row == col >> 1)
@@ -57,9 +60,12 @@
     out_ref[...] = total[:128]
 
 
-def backward(table_ref, tiles_ref, scaled_ref, resid_ref, out_ref, own_ref, total):
+def backward(table_in, tiles_ref, scaled_ref, resid_ref, out_ref, own_ref, total, table_ref, sem):
+    copy = pltpu.make_async_copy(table_in, table_ref, sem)
+    copy.start()
+    total[...] = jnp.zeros_like(total)
+    copy.wait()
     own_ref[...] = resid_ref[pl.ds(number(table_ref, AT_ZH) * 4, 4)]
-    total[...] = jnp.zeros_like(total)
     half = number(table_ref, AT_CORE) << 4
     for i in range(48):
         v, w = number(table_ref, 2 * i), number(table_ref, 2 * i + 1)
@@ -128,9 +134,9 @@
     partial = pl.pallas_call(
         forward,
         out_shape=f32((128, 8, width)),
-        in_specs=[smem, vmem, vmem],
+        in_specs=[vmem, vmem, vmem],
         out_specs=vmem,
-        scratch_shapes=[pltpu.VMEM((136, 8, width), jnp.float32)],
+        scratch_shapes=[pltpu.VMEM((136, 8, width), jnp.float32), pltpu.SMEM((128,), jnp.float32), pltpu.SemaphoreType.DMA],
         compiler_params=params,
         cost_estimate=cost,
     )(table, tiles_here, x_all)
@@ -150,9 +156,9 @@
     back, resid = pl.pallas_call(
         backward,
         out_shape=(jax.ShapeDtypeStruct((64, 8, width), BACK), pltpu.VMEM((4, 8, width), jnp.float32)),
-        in_specs=[smem, vmem, vmem, vmem],
+        in_specs=[vmem, vmem, vmem, vmem],
         out_specs=(vmem, vmem),
-        scratch_shapes=[pltpu.VMEM((72, 8, width), jnp.float32)],
+        scratch_shapes=[pltpu.VMEM((72, 8, width), jnp.float32), pltpu.SMEM((128,), jnp.float32), pltpu.SemaphoreType.DMA],
         compiler_params=params,
         cost_estimate=cost,
     )(table, tiles_here, scaled, resid)

time: 81.8 us -> 81.7 us (level)
  no operation moved by 1% of the time
where the time goes in v9:
time: 81.7 us; the launch traced here: 81.3 us
  blocking collectives  58.6 us (72%)
  starting transfers between devices  9.01 us (11%)
  waiting for transfers between devices  6.47 us (8%)
  Pallas kernels  3.5 us (4%)
  local copies, waits for them, and re-layouts  1.43 us (2%)
  between operations  1.38 us (2%)
  other arithmetic  0.88 us (1%)
    all_gather x2, blocking collectives, gather_pairs(): lax.all_gather(jnp.concatenate([partial, diag], axis=0), 'zh', axis_index...  25.1 us
    all_to_all x1, blocking collectives, body(): lax.all_to_all(back.reshape(16, 4, 8, width), ROW, 0, 0)  10.7 us
    all_to_all x1, blocking collectives, to_all(): return lax.all_to_all(copies, axes, 0, 0)  9.4 us
    all_to_all x1, blocking collectives, body(): partial = jnp.sum(lax.all_to_all(partial, 'y', 0, 0), axis=0)  9.26 us
    all_to_all x1, starting transfers between devices, to_all(): return lax.all_to_all(copies, axes, 0, 0)  9.01 us
    all_to_all x1, waiting for transfers between devices, to_all(): return lax.all_to_all(copies, axes, 0, 0)  6.47 us
    all_gather x1, blocking collectives, body(): halves = lax.all_gather(partial[:, 1], 'c')  4.19 us
    pallas_call x1, Pallas kernels, body(): pl.pallas_call(forward, out_shape=f32((128, 8, width)), in_specs=[vmem, v...  1.67 us
  transfers between devices with their start and end apart: 1, of which 1 were waited for; matrix products, arithmetic and copies ran while one was open for 1% of the time, Pallas kernels for 0%

profile of v9, /device:TPU:1, one launch (start us, length us, event | category | flops | bytes accessed | tf_op | source)
XLA Modules:
  0.0 81.3 jit_solution(16311770423445177575)
XLA Ops:
  0.6 1.4 %broadcast_in_dim.36 = bf16[16,4,8,128]{3,2,1,0:T(8,128)(2,1)} broadcast(bf16[4,8,128]{2,1,0:T(8,128)(2,1)} %bitcast.59), dimensions={1,2,3} | broadcast | bytes 139264 | tf_op jit(solution)/shard_map/broadcast_in_dim | solution.py:89
  2.0 9.0 %all-to-all-start = ((bf16[16,4,8,128]{3,2,1,0:T(8,128)(2,1)}), bf16[16,4,8,128]{3,2,1,0:T(8,128)(2,1)S(1)}, u32[]{:S(2)}, u32[]{:S(2)}) async-start(bf16[16,4,8,128]{3,2,1,0:T(8,128)(2,1)} %broadcast_in_dim.36), calls=%async_computation | async-start | bytes 262144 | tf_op jit(solution)/shard_map/all_to_all | solution.py:90
  11.7 0.8 compare_select_fusion.5.table_ref
  12.4 0.0 copy-start
  12.4 6.5 %all-to-all-done = bf16[16,4,8,128]{3,2,1,0:T(8,128)(2,1)S(1)} async-done(((bf16[16,4,8,128]{3,2,1,0:T(8,128)(2,1)}), bf16[16,4,8,128]{3,2,1,0:T(8,128)(2,1)S(1)}, u32[]{:S(2)}, u32[]{:S(2)}) %all-to-all-start) | async-done | bytes 131104 | tf_op jit(solution)/shard_map/all_to_all | solution.py:90
  18.9 0.0 copy-done
  18.9 0.0 copy-start.1
  18.9 1.7 %shard_map.87 = f32[128,8,128]{2,1,0:T(8,128)S(1)} custom-call(f32[128]{0:T(128)S(1)} %shard_map.86.table_in, bf16[48,256,128]{2,1,0:T(8,128)(2,1)S(1)} %bitcast.45, bf16[64,8,128]{2,1,0:T(8,128)(2,1)S(1)} %bitcast.50), custom_call_target="tpu_custom_call" | custom-call | flops 25165824 | bytes 4194304 | tf_op jit(solution)/shard_map/pallas_call | solution.py:134
  20.6 4.2 %all-gather = f32[8,1,16,8,128]{4,3,2,1,0:T(8,128)S(1)} all-gather(f32[4,1,16,8,128]{4,3,2,1,0:T(8,128)S(1)} %slice.47), channel_id=2, replica_groups=mesh['zl'=4,'x'=4,'y'=4,'zh'=4,'c'=2] {'c'}, dimensions={0}, use_global_device_ids=true | all-gather | bytes 786432 | tf_op jit(solution)/shard_map/all_gather | solution.py:145
  24.9 9.3 %all_to_all.20 = f32[4,16,8,128]{3,2,1,0:T(8,128)S(1)} all-to-all(f32[4,16,8,128]{3,2,1,0:T(8,128)S(1)} %fusion), channel_id=1, replica_groups=mesh['zl'=4,'x'=4,'y'=4,'zh'=4,'c'=2] {'y'}, dimensions={0} | all-to-all | bytes 524288 | tf_op jit(solution)/shard_map/all_to_all | solution.py:147
  34.1 0.0 copy-done.1
  34.2 14.1 %all-gather.1 = f32[34,8,128]{2,1,0:T(8,128)S(1)} all-gather(f32[17,8,128]{2,1,0:T(8,128)S(1)} %select_maximum_fusion), channel_id=3, replica_groups={{0,6},{2,4},{1,7},{3,5},{8,14},{10,12},{9,15},{11,13},{16,22},{18,20},{..., dimensions={0}, use_global_device_ids=true | all-gather | bytes 208896 | tf_op jit(solution)/shard_map/all_gather | solution.py:95
  48.3 11.0 %all-gather.2 = f32[34,8,128]{2,1,0:T(8,128)S(1)} all-gather(f32[17,8,128]{2,1,0:T(8,128)S(1)} %pad_maximum_fusion), channel_id=4, replica_groups={{0,2},{6,4},{1,3},{7,5},{8,10},{14,12},{9,11},{15,13},{16,18},{22,20},{..., dimensions={0}, use_global_device_ids=true | all-gather | bytes 208896 | tf_op jit(solution)/shard_map/all_gather | solution.py:95
  59.4 9.4 %all_to_all.21 = bf16[8,16,8,128]{3,2,1,0:T(8,128)(2,1)S(1)} all-to-all(bf16[8,16,8,128]{3,2,1,0:T(8,128)(2,1)S(1)} %broadcast_in_dim.38), channel_id=1, replica_groups=mesh['zl'=4,'x'=4,'y'=4,'zh'=4,'c'=2] {'y','c'}, dimensions={0} | all-to-all | bytes 524288 | tf_op jit(solution)/shard_map/all_to_all | solution.py:90
  68.8 1.2 %shard_map.88 = (bf16[64,8,128]{2,1,0:T(8,128)(2,1)S(1)}, f32[4,8,128]{2,1,0:T(8,128)S(1)}) custom-call(f32[128]{0:T(128)S(1)} %shard_map.86.table_in, bf16[48,256,128]{2,1,0:T(8,128)(2,1)S(1)} %bitcast.46, bf16[128,8,128]{2,1,0:T(8,128)(2,1)S(1)} %bitcast.49, f32[16,8,128]{2,1,0:T(8,128)S(1)} %get-tuple-element.10.resid_ref), custom_call_target="tpu_custom_call" | custom-call | flops 25165824 | bytes 4194304 | tf_op jit(solution)/shard_map/pallas_call | solution.py:156
  70.0 10.7 %all_to_all.22.parts_ref = bf16[16,4,8,128]{3,2,1,0:T(8,128)(2,1)S(1)} all-to-all(bf16[16,4,8,128]{3,2,1,0:T(8,128)(2,1)S(1)} %bitcast.51), channel_id=1, replica_groups=mesh['zl'=4,'x'=4,'y'=4,'zh'=4,'c'=2] {'zl','x'}, dimensions={0} | all-to-all | bytes 262144 | tf_op jit(solution)/shard_map/all_to_all | solution.py:171
  80.7 0.6 shard_map.89
  (14 shorter events, 0.2 us)
Async XLA Ops:
  2.0 16.9 %all-to-all-start = ((bf16[16,4,8,128]{3,2,1,0:T(8,128)(2,1)}), bf16[16,4,8,128]{3,2,1,0:T(8,128)(2,1)S(1)}, u32[]{:S(2)}, u32[]{:S(2)}) async-start(bf16[16,4,8,128]{3,2,1,0:T(8,128)(2,1)} %broadcast_in_dim.36), calls=%async_computation | async-start | bytes 262144 | tf_op jit(solution)/shard_map/all_to_all | solution.py:90
  12.4 6.5 %copy-start = (bf16[1,1,96,128,128]{4,3,2,1,0:T(8,128)(2,1)S(1)}, bf16[1,1,96,128,128]{4,3,2,1,0:T(8,128)(2,1)}, u32[]{:S(2)}) copy-start(bf16[1,1,96,128,128]{4,3,2,1,0:T(8,128)(2,1)} %param.10) | copy-start | bytes 9437188
  18.9 15.2 %copy-start.1 = (f32[512]{0:T(512)S(1)}, f32[512]{0:T(512)}, u32[]{:S(2)}) copy-start(f32[512]{0:T(512)} %param.8) | copy-start | bytes 6148
